TPU v7x, 128 devices: a whole 4x4x4 slice. The times are simulated.
128 devices in a mesh: group: 8 (over z, core), seq: 16 (over x, y).
Axes of the slice: x: 4, y: 4, z: 4, core: 2. Of those that a mesh axis runs over, the one named last changes fastest.
Arguments:
- queries: bfloat16 [8, 64, 8192], P('group', 'seq'), may hold values from -40 to 40
- prefix_keys: bfloat16 [8, 4, 4, 32768, 128], P('group', None, None, 'seq'), may hold values from -8 to 8
- prefix_values: bfloat16 [8, 4, 4, 32768, 128], P('group', None, None, 'seq'), may hold values from -48 to 48
- cont_keys: bfloat16 [8, 64, 4, 512, 128], P('group', 'seq'), may hold values from -11 to 11
- cont_values: bfloat16 [8, 64, 4, 512, 128], P('group', 'seq'), may hold values from -48 to 48
- cont_len: int32 [8, 64], P('group', 'seq'), may hold values from 1 to 512, as said below
- prompt_of: int32 [8, 64], P('group'), may hold values from 0 to 3, as said below
- w_out: bfloat16 [8192, 4096], P(None, 'group'), may hold values from -0.0625 to 0.0625
Outputs:
- projected: bfloat16 [8, 64, 4096], P('group', 'seq')
Inputs may be any that keep to these rules, and one draw needn't show every extreme that they name: `prompt_of`: within a group each of the 4 prompts is continued by exactly 16 samples. `cont_len`: in every group some sample has 512 live positions.
All inputs are finite; a program needn't handle non-finite values.
Results may differ from a plain program's by a relative error of at most 0.02.
Values may be sent and summed in bfloat16 or wider, within the bound.
No kernel may reach another device: no remote copies, remote signals or barrier semaphores. Data moves between devices by JAX's collectives and lax.ppermute only.
A program may use at most 192 MiB of HBM per device.

v0:
```python
import jax
import jax.numpy as jnp
from jax import lax
from jax.sharding import PartitionSpec as P

HEADS = 64
KVH = 4
HD = 128


def per_device(
    queries, prefix_keys, prefix_values, cont_keys, cont_values, cont_len, prompt_of, w_out
):
    scaling = HD ** (-0.5)
    per_group = HEADS // KVH
    samp_local = queries.shape[1]
    gathered = lax.all_gather(queries, "seq", axis=1, tiled=True)[0]
    samples = gathered.shape[0]
    prompts = prefix_keys.shape[1]
    sorting = jnp.argsort(prompt_of[0], stable=True)
    inverse = jnp.argsort(sorting, stable=True)
    query_sorted = gathered[sorting].reshape(prompts, samples // prompts, KVH, per_group, HD)
    logits = (
        jnp.einsum(
            "pskjd,pktd->pskjt", query_sorted, prefix_keys[0], preferred_element_type=jnp.float32
        )
        * scaling
    )
    maxima = logits.max(-1)
    weights = jnp.exp(logits - maxima[..., None])
    totals = weights.sum(-1)
    carried = jnp.einsum(
        "pskjt,pktd->pskjd",
        weights.astype(jnp.bfloat16),
        prefix_values[0],
        preferred_element_type=jnp.float32,
    )
    pre_summed = carried.reshape(samples, HEADS, HD)[inverse]
    pre_peak = maxima.reshape(samples, HEADS)[inverse]
    pre_total = totals.reshape(samples, HEADS)[inverse]
    offset = lax.axis_index("seq") * samp_local
    highest = lax.pmax(pre_peak, "seq")
    factor = jnp.exp(pre_peak - highest)
    summed_mine, total_mine = (
        lax.psum_scatter(
            (pre_summed * factor[..., None]).astype(jnp.bfloat16),
            "seq",
            scatter_dimension=0,
            tiled=True,
        ).astype(jnp.float32),
        lax.psum_scatter(
            (pre_total * factor).astype(jnp.bfloat16), "seq", scatter_dimension=0, tiled=True
        ).astype(jnp.float32),
    )
    peak_mine = lax.dynamic_slice_in_dim(highest, offset, samp_local, 0)
    query_local = queries[0].reshape(samp_local, KVH, per_group, HD)
    keys_new = cont_keys[0]
    values_new = cont_values[0]
    lengths = cont_len[0]
    cont_max = keys_new.shape[2]
    logits_new = (
        jnp.einsum("skjd,sktd->skjt", query_local, keys_new, preferred_element_type=jnp.float32)
        * scaling
    )
    usable = jnp.arange(cont_max)[None, None, None, :] < lengths[:, None, None, None]
    logits_new = jnp.where(usable, logits_new, -jnp.inf)
    peak_new = logits_new.max(-1)
    weights_new = jnp.exp(logits_new - peak_new[..., None])
    total_new = weights_new.sum(-1)
    summed_new = jnp.einsum(
        "skjt,sktd->skjd",
        weights_new.astype(jnp.bfloat16),
        values_new,
        preferred_element_type=jnp.float32,
    )
    peak_new = peak_new.reshape(samp_local, HEADS)
    total_new = total_new.reshape(samp_local, HEADS)
    summed_new = summed_new.reshape(samp_local, HEADS, HD)
    highest_all = jnp.maximum(peak_mine, peak_new)
    scale_pre = jnp.exp(peak_mine - highest_all)
    scale_new = jnp.exp(peak_new - highest_all)
    numerator = summed_mine * scale_pre[..., None] + summed_new * scale_new[..., None]
    denominator = total_mine * scale_pre + total_new * scale_new
    mixed = (
        (numerator / denominator[..., None]).reshape(1, samp_local, HEADS * HD).astype(jnp.bfloat16)
    )
    columns = jnp.einsum(
        "gsf,fc->gsc",
        lax.all_gather(mixed, "group", axis=0, tiled=True),
        w_out,
        preferred_element_type=jnp.float32,
    ).astype(jnp.bfloat16)
    return lax.all_to_all(columns, "group", split_axis=0, concat_axis=2, tiled=True)


def solution(mesh):
    return jax.shard_map(
        per_device,
        mesh=mesh,
        in_specs=(
            P("group", "seq", None),
            P("group", None, None, "seq", None),
            P("group", None, None, "seq", None),
            P("group", "seq", None, None, None),
            P("group", "seq", None, None, None),
            P("group", "seq"),
            P("group", None),
            P(None, "group"),
        ),
        out_specs=P("group", "seq", None),
        check_vma=False,
    )
```

profile of v0, /device:TPU:32, one launch (start us, length us, event | category | flops | bytes accessed | tf_op | source)
XLA Modules:
  0.0 303.3 jit_solution(79274095089571944)
XLA Ops:
  6.5 0.0 copy-start
  6.5 0.0 all-gather.2.cloned.1.call-start
  6.5 1.7 copy.22
  8.3 0.0 all-gather.2.cloned.1.call-update
  8.3 0.0 reduce-scatter.2.cloned.1.call-start
  8.4 2.7 sort.31
  11.1 2.0 sort.32
  13.1 43.2 %all-gather.2.cloned.1.call-done = bf16[1,64,8192]{2,0,1:T(2,128)(2,1)} async-done(((bf16[1,4,8192]{2,0,1:T(2,128)(2,1)}), bf16[1,64,8192]{2,0,1:T(2,128)(2,1)}) %all-gather.2.cloned.1.call-update) | async-done | bytes 1048592 | tf_op jit(solution)/shard_map/all_gather | solution.py:17
  56.3 2.7 copy.37
  59.1 2.2 gather_fusion
  61.3 1.5 copy.30
  62.8 16.6 %bitcast_reduce_fusion = (f32[4,16,4,16]{3,1,2,0:T(8,128)S(1)}, f32[4,4,16,16,2048]{4,3,2,1,0:T(8,128)}) fusion(bf16[1,4,4,2048,128]{4,3,2,1,0:T(8,128)(2,1)} %param.9, bf16[4,16,4,16,128]{4,3,2,1,0:T(8,128)(2,1)S(1)} %bitcast.79), kind=kOutput, calls=%fused_computation.5 | convolution fusion | flops 2164256768 | bytes 43008000 | tf_op jit(solution)/shard_map/pskjd,pktd->pskjt/dot_general | solution.py:24
  79.3 0.1 copy.25
  79.4 14.0 %fusion.1 = f32[4,16,4,16]{3,1,2,0:T(8,128)S(1)} fusion(f32[4,4,16,16,2048]{4,3,2,1,0:T(8,128)} %get-tuple-element.17, f32[4,16,4,16]{3,1,2,0:T(8,128)S(1)} %get-tuple-element.16), kind=kLoop, calls=%fused_computation.7 | loop fusion | flops 25161728 | bytes 33587200 | tf_op jit(solution)/shard_map/reduce_sum | solution.py:31
  93.4 17.5 %fusion.16 = f32[4,16,4,16,128]{4,3,1,2,0:T(8,128)} fusion(bf16[1,4,4,2048,128]{4,3,2,1,0:T(8,128)(2,1)} %param.10, f32[4,4,16,16,2048]{4,3,2,1,0:T(8,128)} %get-tuple-element.17, f32[4,16,4,16]{3,1,2,0:T(8,128)S(1)} %get-tuple-element.16), kind=kOutput, calls=%fused_computation.22 | convolution fusion | flops 2172649472 | bytes 44056576 | tf_op jit(solution)/shard_map/pskjt,pktd->pskjd/dot_general | solution.py:32
  110.8 0.0 copy-start.1
  110.8 0.0 copy-start.2
  110.8 0.1 reshape.67
  111.0 0.0 copy-start.3
  111.0 3.3 %copy.24 = f32[4,16,4,16,128]{4,3,2,1,0:T(8,128)} copy(f32[4,16,4,16,128]{4,3,1,2,0:T(8,128)} %fusion.16) | data formatting | bytes 4194304 | tf_op jit(solution)/shard_map/pskjt,pktd->pskjd/transpose | solution.py:32
  114.2 0.6 gather_fusion.2
  114.8 3.6 %gather_fusion.1 = f32[64,64,128]{2,1,0:T(8,128)} fusion(f32[64,64,128]{2,1,0:T(8,128)} %bitcast.77, s32[1024]{0:T(1024)S(1)} %pad_clamp_fusion), kind=kCustom, calls=%fused_computation.1 | custom fusion | bytes 4194560 | tf_op jit(solution)/shard_map/gather | solution.py:38
  118.4 0.1 copy.26
  118.4 0.1 reshape.70
  118.6 0.6 gather_fusion.3
  119.2 72.1 %pmax.7 = f32[64,64]{1,0:T(8,128)S(1)} all-reduce(f32[64,64]{1,0:T(8,128)S(1)} %gather_fusion.2), channel_id=1, replica_groups=mesh['group'=8,'seq'=16] {'seq'}, use_global_device_ids=true, to_apply=%region_3.4 | all-reduce | flops 4096 | bytes 32768 | tf_op jit(solution)/shard_map/pmax | solution.py:42
  191.2 2.7 multiply_convert_fusion
  194.0 0.0 reduce-scatter.2.cloned.1.call-update
  194.0 0.0 copy-done.1
  194.0 0.0 copy-done.2
  194.1 0.1 iota_compare_fusion
  194.1 0.0 copy-done
  194.1 0.7 fusion.43
  194.9 0.1 reshape.68
  195.0 0.3 fusion.31
  195.2 0.1 reshape.71
  195.3 0.0 copy-done.3
  195.3 0.6 dynamic-slice
  196.5 2.0 fusion.12
  198.6 69.8 %all-reduce = bf16[64,64]{1,0:T(8,128)(2,1)S(1)} all-reduce(bf16[64,64]{1,0:T(8,128)(2,1)S(1)} %get-tuple-element.12), channel_id=3, replica_groups=mesh['group'=8,'seq'=16] {'seq'}, use_global_device_ids=true, to_apply=%region_7.8.clone | all-reduce | flops 4096 | bytes 16384
  268.4 0.0 reduce-scatter.2.cloned.1.call-done
  268.4 1.0 fusion.37
  269.5 13.3 %all_gather.7 = bf16[8,4,8192]{2,1,0:T(4,128)(2,1)S(1)} all-gather(bf16[1,4,8192]{2,1,0:T(4,128)(2,1)S(1)} %convert_element_type.42), channel_id=1, replica_groups=mesh['group'=8,'seq'=16] {'group'}, dimensions={0}, use_global_device_ids=true | all-gather | bytes 589824 | tf_op jit(solution)/shard_map/all_gather | solution.py:89
  282.7 4.8 %fusion.27 = bf16[8,4,512]{2,1,0:T(4,128)(2,1)S(1)} fusion(bf16[8,4,8192]{2,1,0:T(4,128)(2,1)S(1)} %all_gather.7, bf16[8192,512]{1,0:T(8,128)(2,1)} %param.15), kind=kOutput, calls=%fused_computation.25 | convolution fusion | flops 268451840 | bytes 8945664 | tf_op jit(solution)/shard_map/gsf,fc->gsc/dot_general | solution.py:87
  287.6 8.3 %all_to_all.18 = bf16[8,4,512]{2,1,0:T(4,128)(2,1)S(1)} all-to-all(bf16[8,4,512]{2,1,0:T(4,128)(2,1)S(1)} %fusion.27), channel_id=1, replica_groups=mesh['group'=8,'seq'=16] {'group'}, dimensions={0} | all-to-all | bytes 65536 | tf_op jit(solution)/shard_map/all_to_all | solution.py:93
  295.9 0.6 copy.39
  (10 shorter events, 0.1 us)
Async XLA Ops:
  6.5 187.6 %copy-start = (bf16[1,4,4,512,128]{4,3,2,1,0:T(8,128)(2,1)S(1)}, bf16[1,4,4,512,128]{4,3,2,1,0:T(8,128)(2,1)}, u32[]{:S(2)}) copy-start(bf16[1,4,4,512,128]{4,3,2,1,0:T(8,128)(2,1)} %param.11) | copy-start | bytes 6291460
  6.5 49.8 %all-gather.2.cloned.1.call-start = ((), (), s32[]{:S(2)}) async-start(), calls=%async_computation.2 | async-start | bytes 2228224 | tf_op jit(solution)/shard_map/all_gather | solution.py:17
  8.3 260.1 %reduce-scatter.2.cloned.1.call-start = ((), (), s32[]{:S(2)}) async-start(), calls=%async_computation.3 | async-start | bytes 1114112 | tf_op jit(solution)/shard_map/reduce_scatter | solution.py:45
  110.8 83.2 %copy-start.1 = (bf16[1,4,8192]{2,1,0:T(4,128)(2,1)S(1)}, bf16[1,4,8192]{2,1,0:T(4,128)(2,1)}, u32[]{:S(2)}) copy-start(bf16[1,4,8192]{2,1,0:T(4,128)(2,1)} %param.8) | copy-start | bytes 196612
  110.8 83.2 %copy-start.2 = (s32[1,4]{1,0:T(1,128)S(1)}, s32[1,4]{1,0:T(1,128)}, u32[]{:S(2)}) copy-start(s32[1,4]{1,0:T(1,128)} %param.13) | copy-start | bytes 52
  111.0 84.3 %copy-start.3 = (u32[128]{0:T(128)S(1)}, u32[128]{0:T(128)}, u32[]{:S(2)}) copy-start(u32[128]{0:T(128)} %constant.28) | copy-start | bytes 1540
Sparse Core Ops, SparseCore 0:
  9.5 46.7 all-gather.1
  194.1 69.1 reduce-scatter.1
where the time goes:
time: 306 us; the launch traced here: 303 us
  blocking collectives  163 us (53%)
  waiting for transfers between devices  43.3 us (14%)
  matrix products  41.6 us (14%)
  other arithmetic  22.8 us (7%)
  local copies, waits for them, and re-layouts  18 us (6%)
  between operations  14.2 us (5%)
    pmax x1, blocking collectives, per_device(): highest = lax.pmax(pre_peak, 'seq')  72.1 us
    unnamed x1, blocking collectives  69.8 us
    all_gather x1, waiting for transfers between devices, per_device(): gathered = lax.all_gather(queries, 'seq', axis=1, tiled=True)[0]  43.2 us
    dot_general x1, matrix products, per_device(): jnp.einsum('pskjt,pktd->pskjd', weights.astype(jnp.bfloat16), prefix_valu...  17.5 us
    dot_general x1, matrix products, per_device(): jnp.einsum('pskjd,pktd->pskjt', query_sorted, prefix_keys[0], preferred_e...  16.6 us
    reduce_sum x1, other arithmetic, per_device(): totals = weights.sum(-1)  14 us
    all_gather x1, blocking collectives, per_device(): lax.all_gather(mixed, 'group', axis=0, tiled=True)  13.3 us
    all_to_all x1, blocking collectives, per_device(): lax.all_to_all(columns, 'group', split_axis=0, concat_axis=2, tiled=True)  8.3 us
  transfers between devices with their start and end apart: 2, of which 1 were waited for; matrix products, arithmetic and copies ran while one was open for 3% of the time, Pallas kernels for 0%

commit v1 on v0

v1 whole, which is shorter than its diff:
```python
import functools

import jax
import jax.numpy as jnp
import numpy as np
from jax import lax
from jax.experimental import pallas as pl
from jax.experimental.pallas import tpu as pltpu
from jax.sharding import PartitionSpec as P

HEADS = 64
KVH = 4
HD = 128
PER = HEADS // KVH
PROMPTS = 4
SAMP = 16
CHUNKS = 2
KC = KVH // CHUNKS
HC = HEADS // CHUNKS
T_LOCAL = 2048
CONT = 512
D = 4096
LOG2E = float(np.log2(np.e))
SCALE2 = float(np.log2(np.e) / np.sqrt(HD))
BF = jnp.bfloat16
F32 = jnp.float32
VMEM = pl.BlockSpec(memory_space=pltpu.VMEM)
SMEM = pl.BlockSpec(memory_space=pltpu.SMEM)
ANY = pl.BlockSpec(memory_space=pl.ANY)

SWAP = np.zeros((256, 256), np.float32)
for _j in range(16):
    for _i in range(16):
        SWAP[16 * _j + _i, 16 * _i + _j] = 1


def dot(a, b):
    return jnp.dot(a, b, preferred_element_type=F32)


def dot_t(a, b):
    return lax.dot_general(a, b, (((1,), (1,)), ((), ())), preferred_element_type=F32)


def split3(x):
    hi = x.astype(BF).astype(F32)
    mid = (x - hi).astype(BF).astype(F32)
    return hi, mid, x - hi - mid


def iota(shape, dim):
    return lax.broadcasted_iota(jnp.int32, shape, dim)


def cont_kernel(len_ref, q_ref, k_hbm, v_hbm, tail_ref, kb, vb, sem):
    def copies(s):
        return (
            pltpu.make_async_copy(k_hbm.at[s], kb.at[s], sem.at[s, 0]),
            pltpu.make_async_copy(v_hbm.at[s], vb.at[s], sem.at[s, 1]),
        )

    for s in range(4):
        for c in copies(s):
            c.start()
    tail_ref[...] = jnp.zeros_like(tail_ref)
    lane = iota((16, 128), 1)
    row = iota((16, 128), 0)
    logs = [jnp.zeros((8, 128), F32) for _ in range(KVH)]
    for s in range(4):
        for c in copies(s):
            c.wait()
        live = iota((16, CONT), 1) < len_ref[s]
        for k in range(KVH):
            logit = jnp.where(live, dot_t(q_ref[s, 16 * k : 16 * k + 16], kb[s, k]), -jnp.inf)
            top = logit.max(1, keepdims=True)
            w = jnp.exp2((logit - top) * SCALE2)
            total = w.sum(1, keepdims=True)
            o = dot(w.astype(BF), vb[s, k]) * (1.0 / total)
            lse = top * SCALE2 + jnp.log(total) * LOG2E
            c, kk = k // KC, k % KC
            for j in range(16):
                tail_ref[c, 8 * kk + j // 2, (j % 2) * 4 + s : (j % 2) * 4 + s + 1, :] = o[j : j + 1]
            spread = jnp.where(lane == (row % 2) * 4 + s, jnp.broadcast_to(lse, (16, 128)), 0.0)
            logs[k] = logs[k] + spread.reshape(8, 2, 128).sum(1)
    for k in range(KVH):
        c, kk = k // KC, k % KC
        for n, part in enumerate(split3(logs[k])):
            for d in range(8):
                tail_ref[c, 8 * kk + d, 11 + n : 12 + n, :] = part[d : d + 1]


def cont_call(lengths, q, keys, values):
    return pl.pallas_call(
        cont_kernel,
        out_shape=jax.ShapeDtypeStruct((CHUNKS, 16, 16, 128), F32),
        in_specs=[SMEM, VMEM, ANY, ANY],
        out_specs=VMEM,
        scratch_shapes=[
            pltpu.VMEM((4, KVH, CONT, HD), BF),
            pltpu.VMEM((4, KVH, CONT, HD), BF),
            pltpu.SemaphoreType.DMA((4, 2)),
        ],
        compiler_params=pltpu.CompilerParams(vmem_limit_bytes=60 * 2**20),
        cost_estimate=pl.CostEstimate(flops=2 * 10**8, bytes_accessed=2**22, transcendentals=131072),
        name="cont",
    )(lengths, q, keys, values)


NB = KC * PROMPTS
TC = 512


def prefix_kernel(chunk, order, q_hbm, swap_ref, tail_ref, k_hbm, v_hbm, o_ref, qv, qs, kb, vb, sbuf, st, qsem, ks, vs):
    cq = pltpu.make_async_copy(q_hbm.at[:, KC * chunk : KC * chunk + KC], qv, qsem)
    cq.start()

    def copies(b):
        kq, p = b // PROMPTS, b % PROMPTS
        return (
            pltpu.make_async_copy(k_hbm.at[p, KC * chunk + kq], kb.at[b], ks.at[b]),
            pltpu.make_async_copy(v_hbm.at[p, KC * chunk + kq], vb.at[b], vs.at[b]),
        )

    for b in range(NB):
        for c in copies(b):
            c.start()
    cq.wait()
    for b in range(NB):
        kq, p = b // PROMPTS, b % PROMPTS
        for i in range(SAMP):
            qs[b, 16 * i : 16 * i + 16] = qv[order[16 * p + i], kq]
        qs[b] = dot(swap_ref[...], qs[b]).astype(BF)

    row = iota((256, 128), 0) % 32
    lane = iota((256, 128), 1)

    def finish(b, o, top, total):
        kq, p = b // PROMPTS, b % PROMPTS
        o = (o * (1.0 / total)).astype(BF)
        o_ref[8 * kq : 8 * kq + 8, 32 * p : 32 * p + 32, :] = o.reshape(8, 32, 128)
        lse = top * SCALE2 + jnp.log(total) * LOG2E
        spread = jnp.where(lane == p * 32 + row, jnp.broadcast_to(lse, (256, 128)), 0.0)
        spread = spread.reshape(8, 32, 128).sum(1)
        if p == 0:
            st[kq] = spread
        else:
            st[kq] = st[kq] + spread

    prev_top = None
    for b in range(NB + 1):
        peak = None
        if b < NB:
            for c in copies(b):
                c.wait()
            q = qs[b]
        if b > 0:
            acc = total = None
        for t in range(T_LOCAL // TC):
            cols = slice(t * TC, (t + 1) * TC)
            if b < NB:
                s = dot_t(q, kb[b, cols])
                sbuf[b % 2, :, cols] = s
                for z in range(TC // 128):
                    piece = s[:, 128 * z : 128 * z + 128]
                    peak = piece if peak is None else jnp.maximum(peak, piece)
            if b > 0:
                w = jnp.exp2((sbuf[(b - 1) % 2, :, cols] - prev_top) * SCALE2)
                for z in range(TC // 128):
                    piece = w[:, 128 * z : 128 * z + 128]
                    total = piece if total is None else total + piece
                o = dot(w.astype(BF), vb[b - 1, cols])
                acc = o if acc is None else acc + o
        if b > 0:
            finish(b - 1, acc, prev_top, total.sum(1, keepdims=True))
        if b < NB:
            prev_top = peak.max(1, keepdims=True)
    for kq in range(KC):
        parts = split3(st[kq])
        for d in range(8):
            dest = 8 * kq + d
            tail_ref[0, dest, 8:9, :] = parts[0][d : d + 1]
            tail_ref[0, dest, 9:10, :] = parts[1][d : d + 1]
            tail_ref[0, dest, 10:11, :] = parts[2][d : d + 1]
    o_ref[:, 128:144, :] = tail_ref[0].astype(BF)


def prefix_body(chunk, order, q_hbm, swap_ref, tail_in, k_hbm, v_hbm, o_ref, tail, *rest):
    tail[...] = tail_in[chunk : chunk + 1]
    prefix_kernel(chunk, order, q_hbm, swap_ref, tail, k_hbm, v_hbm, o_ref, *rest)


def prefix_call(chunk, order, q, swap, tail, keys, values):
    return pl.pallas_call(
        functools.partial(prefix_body, chunk),
        out_shape=jax.ShapeDtypeStruct((16, 144, 128), BF),
        in_specs=[SMEM, ANY, VMEM, VMEM, ANY, ANY],
        out_specs=VMEM,
        scratch_shapes=[
            pltpu.VMEM((1, 16, 16, 128), F32),
            pltpu.VMEM((64, KC, 16, 128), BF),
            pltpu.VMEM((NB, 256, 128), BF),
            pltpu.VMEM((NB, T_LOCAL, HD), BF),
            pltpu.VMEM((NB, T_LOCAL, HD), BF),
            pltpu.VMEM((2, 256, T_LOCAL), F32),
            pltpu.VMEM((KC, 8, 128), F32),
            pltpu.SemaphoreType.DMA,
            pltpu.SemaphoreType.DMA((NB,)),
            pltpu.SemaphoreType.DMA((NB,)),
        ],
        compiler_params=pltpu.CompilerParams(vmem_limit_bytes=60 * 2**20),
        cost_estimate=pl.CostEstimate(flops=4 * 10**9, bytes_accessed=9 * 2**20, transcendentals=2**22),
        name=f"prefix{chunk}",
    )(order, q, swap, tail, keys, values)


def project_kernel(chunk, col_ref, r_ref, pm_ref, u_ref, *refs):
    last = chunk == CHUNKS - 1
    w_hbm, refs = refs[:8], refs[8:]
    if chunk:
        prev_ref, refs = refs[0], refs[1:]
    out_ref, wv, sem = refs[0], refs[-2], refs[-1]
    loads = [pltpu.make_async_copy(w_hbm[n].at[chunk], wv.at[n], sem.at[n]) for n in range(8)]
    for load in loads:
        load.start()
    f = lambda x: x.astype(F32)
    lp = f(r_ref[:, 136]) + f(r_ref[:, 137]) + f(r_ref[:, 138])
    lp = jnp.transpose(jnp.concatenate([lp, jnp.zeros((112, 128), F32)], 0))
    lane = iota((128, 128), 1)
    row = iota((128, 128), 0)
    cont = f(r_ref[:, 128:136]).reshape(128, 128)
    cols = jnp.zeros((128, 128), F32)
    for n in range(3):
        piece = jnp.broadcast_to(f(r_ref[:, 139 + n])[:, None, :], (16, 8, 128)).reshape(128, 128)
        piece = jnp.where(lane == row % 8, piece, 0.0).sum(1, keepdims=True)
        cols = cols + jnp.where(lane == n, jnp.broadcast_to(piece, (128, 128)), 0.0)
    moved = dot(pm_ref[...], jnp.concatenate([cont, cols], 1).astype(BF))
    lc = moved[:, 128:129] + moved[:, 129:130] + moved[:, 130:131]
    top = jnp.maximum(jnp.where(lane < 16, lp, -jnp.inf).max(1, keepdims=True), lc)
    wc = jnp.exp2(lc - top)
    wp = jnp.where(lane < 16, jnp.exp2(jnp.where(lane < 16, lp, top) - top), 0.0)
    den = wp.sum(1, keepdims=True) + wc
    num = wc * moved[:, :128]
    for src in range(16):
        num = num + wp[:, src : src + 1] * f(r_ref[src, :128])
    mixed = (num / den).astype(BF).reshape(4, 2, 16, 128)
    mixed = jnp.concatenate([mixed[:, 0].reshape(64, 128), mixed[:, 1].reshape(64, 128)], 1)
    mixed = dot(u_ref[...], mixed).astype(BF)
    y_ref = refs[1] if last else out_ref
    for n in range(8):
        at = pl.ds(pl.multiple_of(col_ref[n] * 512, 512), 512)
        loads[n].wait()
        y = dot(mixed, wv[n])
        if chunk:
            y = y + prev_ref[:, at]
        y_ref[:, at] = y
    if last:
        zf = refs[2]
        for quarter in range(4):
            block = y_ref[:, 1024 * quarter : 1024 * quarter + 1024]
            for dest in range(16):
                zf[dest, 4 * quarter : 4 * quarter + 4, :] = block[4 * dest : 4 * dest + 4]
        out_ref[...] = zf[...].astype(BF)


def project_call(chunk, columns, received, pm, unsort, weights, prev):
    args = (columns, received, pm, unsort, *weights) + ((prev,) if chunk else ())
    last = chunk == CHUNKS - 1
    scratch = [pltpu.VMEM((8, 2 * HD, 512), BF), pltpu.SemaphoreType.DMA((8,))]
    if last:
        out_shape = jax.ShapeDtypeStruct((16, 16, 1024), BF)
        scratch = [pltpu.VMEM((64, D), F32), pltpu.VMEM((16, 16, 1024), F32)] + scratch
    else:
        out_shape = jax.ShapeDtypeStruct((64, D), F32)
    return pl.pallas_call(
        functools.partial(project_kernel, chunk),
        out_shape=out_shape,
        in_specs=[SMEM, VMEM, VMEM, VMEM] + [ANY] * 8 + [VMEM] * (chunk > 0),
        out_specs=VMEM,
        scratch_shapes=scratch,
        compiler_params=pltpu.CompilerParams(vmem_limit_bytes=60 * 2**20),
        cost_estimate=pl.CostEstimate(flops=3 * 10**8, bytes_accessed=4 * 2**20, transcendentals=2**15),
        name=f"project{chunk}",
    )(*args)


def sum_kernel(r_ref, o_ref):
    total = r_ref[0].astype(F32)
    for src in range(1, 16):
        total = total + r_ref[src].astype(F32)
    for quarter in range(4):
        o_ref[:, 1024 * quarter : 1024 * quarter + 1024] = total[4 * quarter : 4 * quarter + 4].astype(BF)


def sum_call(received):
    return pl.pallas_call(
        sum_kernel,
        out_shape=jax.ShapeDtypeStruct((4, D), BF),
        in_specs=[VMEM],
        out_specs=VMEM,
        name="sum",
    )(received)


def spread_weights(w_out, seq):
    own = [
        lax.dynamic_slice_in_dim(w_out, (HC * c + 2 * seq) * HD, 2 * HD, 0) for c in range(CHUNKS)
    ]
    own = lax.optimization_barrier(jnp.stack(own))
    member = lax.axis_index("group")
    z, core = member // 2, member % 2
    blocks, columns = [own], [member]
    for k in (1, 2, 3):
        hop = [(2 * a + c, 2 * ((a + k) % 4) + c) for a in range(4) for c in range(2)]
        blocks.append(lax.ppermute(own, "group", hop))
        columns.append(2 * ((z - k) % 4) + core)
    swap = [(j, j ^ 1) for j in range(8)]
    blocks += [lax.ppermute(b, "group", swap) for b in blocks]
    columns += [c + 1 - 2 * core for c in columns]
    return blocks, jnp.stack(columns).astype(jnp.int32)


def per_device(
    queries, prefix_keys, prefix_values, cont_keys, cont_values, cont_len, prompt_of, w_out
):
    seq = lax.axis_index("seq")
    q = queries[0].reshape(4, HEADS, HD)
    q_rows = q.reshape(4 * HEADS, HD)
    copies = jnp.broadcast_to(q_rows[None], (16, 4 * HEADS, HD))
    copies, w_out = lax.optimization_barrier((copies, w_out))
    gathered = lax.all_to_all(copies, "seq", 0, 0).reshape(64, KVH, PER, HD)

    prompt = prompt_of[0]
    same = prompt[:, None] == prompt[None, :]
    earlier = jnp.arange(64)[None, :] < jnp.arange(64)[:, None]
    pos = prompt * SAMP + jnp.sum(same & earlier, axis=1, dtype=jnp.int32)
    unsort = pos[:, None] == jnp.arange(64)[None, :]
    order = jnp.sum(jnp.where(unsort, jnp.arange(64)[:, None], 0), axis=0, dtype=jnp.int32)
    r = jnp.arange(128)
    r_pos = (r // 32) * 16 + r % 16
    r_jj = (r // 16) % 2
    c_jj = (r // 4) % 2
    c_pos = jnp.repeat(pos.reshape(16, 1, 4), 2, axis=1).reshape(128)
    pm = ((r_pos[:, None] == c_pos[None, :]) & (r_jj[:, None] == c_jj[None, :])).astype(BF)
    unsort = unsort.astype(BF)
    swap = jnp.asarray(SWAP, BF)

    weights, columns = spread_weights(w_out, seq)
    tail = cont_call(cont_len[0], q, cont_keys[0], cont_values[0])
    received = []
    for c in range(CHUNKS):
        part = prefix_call(c, order, gathered, swap, tail, prefix_keys[0], prefix_values[0])
        received.append(lax.all_to_all(part, "seq", 0, 0))
    y = None
    for c in range(CHUNKS):
        y = project_call(c, columns, received[c], pm, unsort, weights, y)
    z = lax.all_to_all(y, "seq", 0, 0)
    return sum_call(z)[None]


def solution(mesh):
    return jax.shard_map(
        per_device,
        mesh=mesh,
        in_specs=(
            P("group", "seq", None),
            P("group", None, None, "seq", None),
            P("group", None, None, "seq", None),
            P("group", "seq", None, None, None),
            P("group", "seq", None, None, None),
            P("group", "seq"),
            P("group", None),
            P(None, "group"),
        ),
        out_specs=P("group", "seq", None),
        check_vma=False,
    )
```

time: 306 us -> 104 us (0.34)
  blocking collectives: 163 us -> 14.3 us
  Pallas kernels: 0 us -> 43.7 us
  matrix products: 41.6 us -> 0 us
  waiting for transfers between devices: 43.3 us -> 6.11 us
  starting transfers between devices: 0.04 us -> 27.6 us
  other arithmetic: 22.8 us -> 3.06 us
  between operations: 14.2 us -> 0.24 us
  local copies, waits for them, and re-layouts: 18 us -> 8.25 us
    pmax x1 -> x0, blocking collectives: 72.1 us -> none  [per_device(): highest = lax.pmax(pre_peak, 'seq')]
    unnamed x1 -> x0, blocking collectives: 69.8 us -> none
    pallas_call x0 -> x6, Pallas kernels: none -> 43.7 us  [the longest x2 24.9 us: prefix_call(): pl.pallas_call(functools.partial(prefix_body, chunk), out_shape=jax.Shape...]
    all_gather x1 -> x0, waiting for transfers between devices: 43.2 us -> none  [per_device(): gathered = lax.all_gather(queries, 'seq', axis=1, tiled=True)[0]]
    dot_general x5 -> x0, matrix products: 41.6 us -> none  [the longest x1 17.5 us: per_device(): jnp.einsum('pskjt,pktd->pskjd', weights.astype(jnp.bfloat16), prefix_valu...]
    all_to_all x0 -> x3, starting transfers between devices: none -> 21 us  [the longest x2 14 us: per_device(): received.append(lax.all_to_all(part, 'seq', 0, 0))]
    all_gather x1 -> x0, blocking collectives: 13.3 us -> none  [per_device(): lax.all_gather(mixed, 'group', axis=0, tiled=True)]
    reduce_sum x2, other arithmetic: 14.3 us -> 1.57 us  [the longest x1 0.91 us: per_device(): pos = prompt * SAMP + jnp.sum(same & earlier, axis=1, dtype=jnp.int32)]
  transfers between devices with their start and end apart: 2 -> 10, of which waited for: 1 -> 2; matrix products, arithmetic and copies ran while one was open for 3% -> 6% of each run, Pallas kernels for 0% -> 36%
where the time goes in v1:
time: 104 us; the launch traced here: 103 us
  Pallas kernels  43.7 us (42%)
  starting transfers between devices  27.6 us (27%)
  blocking collectives  14.3 us (14%)
  local copies, waits for them, and re-layouts  8.25 us (8%)
  waiting for transfers between devices  6.11 us (6%)
  other arithmetic  3.06 us (3%)
    pallas_call x2, Pallas kernels, prefix_call(): pl.pallas_call(functools.partial(prefix_body, chunk), out_shape=jax.Shape...  24.9 us
    all_to_all x1, blocking collectives, per_device(): z = lax.all_to_all(y, 'seq', 0, 0)  14.3 us
    all_to_all x2, starting transfers between devices, per_device(): received.append(lax.all_to_all(part, 'seq', 0, 0))  14 us
    pallas_call x2, Pallas kernels, project_call(): pl.pallas_call(functools.partial(project_kernel, chunk), out_shape=out_sh...  9.95 us
    pallas_call x1, Pallas kernels, cont_call(): pl.pallas_call(cont_kernel, out_shape=jax.ShapeDtypeStruct((CHUNKS, 16, 1...  7.1 us
    all_to_all x1, starting transfers between devices, per_device(): gathered = lax.all_to_all(copies, 'seq', 0, 0).reshape(64, KVH, PER, HD)  7.03 us
    ppermute x3, starting transfers between devices, spread_weights(): blocks.append(lax.ppermute(own, 'group', hop))  5.68 us
    all_to_all x2, waiting for transfers between devices, per_device(): received.append(lax.all_to_all(part, 'seq', 0, 0))  5.6 us
  transfers between devices with their start and end apart: 10, of which 2 were waited for; matrix products, arithmetic and copies ran while one was open for 6% of the time, Pallas kernels for 36%

profile of v1, /device:TPU:32, one launch (start us, length us, event | category | flops | bytes accessed | tf_op | source)
XLA Modules:
  0.0 103.3 jit_solution(3753238598512744101)
XLA Ops:
  0.0 0.0 copy-start.6
  0.0 0.9 broadcast_in_dim.19
  0.9 1.2 %broadcast_in_dim.20 = bf16[16,256,128]{2,1,0:T(8,128)(2,1)} broadcast(bf16[256,128]{1,0:T(8,128)(2,1)S(1)} %broadcast_in_dim.19), dimensions={1,2} | broadcast | bytes 1114112 | tf_op jit(solution)/shard_map/broadcast_in_dim | solution.py:328
  2.1 7.0 %all-to-all-start = ((bf16[16,256,128]{2,1,0:T(8,128)(2,1)}), bf16[16,256,128]{2,1,0:T(8,128)(2,1)S(1)}, u32[]{:S(2)}, u32[]{:S(2)}) async-start(bf16[16,256,128]{2,1,0:T(8,128)(2,1)} %broadcast_in_dim.20), calls=%async_computation | async-start | bytes 2097152 | tf_op jit(solution)/shard_map/all_to_all | solution.py:330
  9.2 1.1 %dynamic-slice_bitcast_fusion.1 = (bf16[1,256,512]{2,1,0:T(8,128)(2,1)S(1)}, bf16[1,256,512]{2,1,0:T(8,128)(2,1)S(1)}) fusion(bf16[8192,512]{1,0:T(8,128)(2,1)} %param.16, s32[]{:T(128)S(6)} %select_n.94, s32[]{:T(128)S(6)} %select_n.95), kind=kLoop, calls=%fused_computation.2 | loop fusion | bytes 1048584 | tf_op jit(solution)/shard_map/stack | solution.py:308
  10.2 0.1 pad_maximum_fusion.refs_0_
  10.3 0.0 copy-start.1
  10.3 0.1 collective-permute-start.3
  10.4 0.2 collective-permute-start.2
  10.6 3.3 %collective-permute-start.1 = (bf16[2,256,512]{2,1,0:T(8,128)(2,1)S(1)}, bf16[2,256,512]{2,1,0:T(8,128)(2,1)}, u32[]{:S(2)}, u32[]{:S(2)}) collective-permute-start(bf16[2,256,512]{2,1,0:T(8,128)(2,1)S(1)} %pad_maximum_fusion.refs_0_), channel_id=1, source_target_pairs={{0,64},{16,80},{32,96},{48,112},{64,0},{80,16},{96,32},{112,48},{1... | collective-permute-start | bytes 1572872 | tf_op jit(solution)/shard_map/ppermute | solution.py:314
  13.9 2.2 %collective-permute-start = (bf16[2,256,512]{2,1,0:T(8,128)(2,1)S(1)}, bf16[2,256,512]{2,1,0:T(8,128)(2,1)}, u32[]{:S(2)}, u32[]{:S(2)}) collective-permute-start(bf16[2,256,512]{2,1,0:T(8,128)(2,1)S(1)} %pad_maximum_fusion.refs_0_), channel_id=1, source_target_pairs={{0,32},{16,48},{32,64},{48,80},{64,96},{80,112},{96,0},{112,16},{1... | collective-permute-start | bytes 1572872 | tf_op jit(solution)/shard_map/ppermute | solution.py:314
  16.1 0.9 convert_reduce_fusion
  17.0 0.1 reduce_sum.22
  17.1 1.5 %copy.12 = bf16[1,4,64,128]{3,2,1,0:T(8,128)(2,1)} copy(bf16[1,4,64,128]{3,1,2,0:T(4,128)(2,1)} %bitcast.37) | data formatting | bytes 131072
  18.6 7.1 %cont.1.tail_in = f32[2,16,16,128]{3,2,1,0:T(8,128)} custom-call(s32[4]{0:T(128)} %bitcast.38, bf16[4,64,128]{2,1,0:T(8,128)(2,1)} %bitcast.36, bf16[4,4,512,128]{3,2,1,0:T(8,128)(2,1)} %bitcast.34, bf16[4,4,512,128]{3,2,1,0:T(8,128)(2,1)} %bitcast.35), custom_call_target="tpu_custom_call" | custom-call | flops 200000000 | bytes 4194304 | tf_op jit(solution)/shard_map/cont/pallas_call | solution.py:93
  25.7 0.0 copy-done.6
  25.7 0.7 select_reduce_fusion.order
  26.4 0.5 all-to-all-done
  26.9 0.0 copy-start
  26.9 1.0 copy-done
  27.8 12.5 %prefix0.1 = bf16[16,144,128]{2,1,0:T(8,128)(2,1)} custom-call(s32[64]{0:T(128)} %select_reduce_fusion.order, bf16[64,4,16,128]{3,2,1,0:T(8,128)(2,1)} %bitcast.32, bf16[256,256]{1,0:T(8,128)(2,1)} %constant.130.clone.swap_ref, f32[2,16,16,128]{3,2,1,0:T(8,128)} %cont.1.tail_in, bf16[4,4,2048,128]{3,2,1,0:T(8,128)(2,1)} %bitcast.28, ...), custom_call_target="tpu_custom_call" | custom-call | flops 4000000000 | bytes 9437184 | tf_op jit(solution)/shard_map/prefix0/pallas_call | solution.py:193
  40.3 0.0 copy-done.1
  40.3 6.7 %all-to-all-start.2 = ((bf16[16,144,128]{2,1,0:T(8,128)(2,1)}), bf16[16,144,128]{2,1,0:T(8,128)(2,1)S(1)}, u32[]{:S(2)}, u32[]{:S(2)}) async-start(bf16[16,144,128]{2,1,0:T(8,128)(2,1)} %prefix0.1), calls=%async_computation.2 | async-start | bytes 1179648 | tf_op jit(solution)/shard_map/all_to_all | solution.py:352
  47.1 0.1 mul.64
  47.2 0.1 eq.67
  47.3 0.7 stack.44.col_ref
  48.0 0.0 collective-permute-done.2.refs_3_
  48.0 0.0 copy-start.5
  48.0 0.1 collective-permute-start.6
  48.1 0.0 collective-permute-done.1.refs_2_
  48.1 0.5 collective-permute-start.5
  48.6 0.0 collective-permute-done.refs_1_
  48.6 0.3 collective-permute-start.4
  48.9 12.5 %prefix1.1 = bf16[16,144,128]{2,1,0:T(8,128)(2,1)} custom-call(s32[64]{0:T(128)} %select_reduce_fusion.order, bf16[64,4,16,128]{3,2,1,0:T(8,128)(2,1)} %bitcast.33, bf16[256,256]{1,0:T(8,128)(2,1)} %constant.130.clone.swap_ref, f32[2,16,16,128]{3,2,1,0:T(8,128)} %cont.1.tail_in, bf16[4,4,2048,128]{3,2,1,0:T(8,128)(2,1)} %bitcast.29, ...), custom_call_target="tpu_custom_call" | custom-call | flops 4000000000 | bytes 9437184 | tf_op jit(solution)/shard_map/prefix1/pallas_call | solution.py:193
  61.3 0.0 copy-done.5
  61.3 0.0 all-to-all-done.2.r_ref
  61.3 0.0 copy-start.2
  61.4 7.2 %all-to-all-start.1 = ((bf16[16,144,128]{2,1,0:T(8,128)(2,1)}), bf16[16,144,128]{2,1,0:T(8,128)(2,1)S(1)}, u32[]{:S(2)}, u32[]{:S(2)}) async-start(bf16[16,144,128]{2,1,0:T(8,128)(2,1)} %prefix1.1), calls=%async_computation.1 | async-start | bytes 1179648 | tf_op jit(solution)/shard_map/all_to_all | solution.py:352
  68.6 0.7 fusion.u_ref
  69.3 0.7 and_convert_fusion.pm_ref
  70.0 0.0 collective-permute-done.3.refs_4_
  70.0 0.0 copy-start.4
  70.0 0.0 collective-permute-done.6.refs_7_
  70.0 0.0 collective-permute-done.5.refs_6_
  70.0 0.0 collective-permute-done.4.refs_5_
  70.0 0.0 copy-done.2
  70.0 0.8 copy-done.4
  70.8 4.8 %project0.1.refs_8_ = f32[64,4096]{1,0:T(8,128)} custom-call(s32[8]{0:T(128)} %stack.44.col_ref, bf16[16,144,128]{2,1,0:T(8,128)(2,1)} %copy-done.2, bf16[128,128]{1,0:T(8,128)(2,1)} %and_convert_fusion.pm_ref, bf16[64,64]{1,0:T(8,128)(2,1)} %fusion.u_ref, bf16[2,256,512]{2,1,0:T(8,128)(2,1)} %copy-done.1, ...), custom_call_target="tpu_custom_call" | custom-call | flops 300000000 | bytes 4194304 | tf_op jit(solution)/shard_map/project0/pallas_call | solution.py:274
  75.6 5.6 %all-to-all-done.1.r_ref = bf16[16,144,128]{2,1,0:T(8,128)(2,1)S(1)} async-done(((bf16[16,144,128]{2,1,0:T(8,128)(2,1)}), bf16[16,144,128]{2,1,0:T(8,128)(2,1)S(1)}, u32[]{:S(2)}, u32[]{:S(2)}) %all-to-all-start.1) | async-done | bytes 589856 | tf_op jit(solution)/shard_map/all_to_all | solution.py:352
  81.2 0.0 copy-start.3
  81.2 0.8 copy-done.3
  82.0 5.2 %project1.1 = bf16[16,16,1024]{2,1,0:T(8,128)(2,1)} custom-call(s32[8]{0:T(128)} %stack.44.col_ref, bf16[16,144,128]{2,1,0:T(8,128)(2,1)} %copy-done.3, bf16[128,128]{1,0:T(8,128)(2,1)} %and_convert_fusion.pm_ref, bf16[64,64]{1,0:T(8,128)(2,1)} %fusion.u_ref, bf16[2,256,512]{2,1,0:T(8,128)(2,1)} %copy-done.1, ...), custom_call_target="tpu_custom_call" | custom-call | flops 300000000 | bytes 4194304 | tf_op jit(solution)/shard_map/project1/pallas_call | solution.py:274
  87.2 14.3 %all_to_all.20.r_ref = bf16[16,16,1024]{2,1,0:T(8,128)(2,1)} all-to-all(bf16[16,16,1024]{2,1,0:T(8,128)(2,1)} %project1.1), channel_id=1, replica_groups=mesh['group'=8,'seq'=16] {'seq'}, dimensions={0} | all-to-all | bytes 1048576 | tf_op jit(solution)/shard_map/all_to_all | solution.py:356
  101.6 1.7 %sum.1 = bf16[4,4096]{1,0:T(4,128)(2,1)} custom-call(bf16[16,16,1024]{2,1,0:T(8,128)(2,1)} %all_to_all.20.r_ref), custom_call_target="tpu_custom_call" | custom-call | tf_op jit(solution)/shard_map/sum/pallas_call | solution.py:295
  (6 shorter events, 0.0 us)
Async XLA Ops:
  0.0 25.7 %copy-start.6 = (s32[1,64]{1,0:T(1,128)S(1)}, s32[1,64]{1,0:T(1,128)}, u32[]{:S(2)}) copy-start(s32[1,64]{1,0:T(1,128)} %param.15) | copy-start | bytes 772
  2.1 24.7 %all-to-all-start = ((bf16[16,256,128]{2,1,0:T(8,128)(2,1)}), bf16[16,256,128]{2,1,0:T(8,128)(2,1)S(1)}, u32[]{:S(2)}, u32[]{:S(2)}) async-start(bf16[16,256,128]{2,1,0:T(8,128)(2,1)} %broadcast_in_dim.20), calls=%async_computation | async-start | bytes 2097152 | tf_op jit(solution)/shard_map/all_to_all | solution.py:330
  10.3 30.0 %copy-start.1 = (bf16[2,256,512]{2,1,0:T(8,128)(2,1)}, bf16[2,256,512]{2,1,0:T(8,128)(2,1)S(1)}, u32[]{:S(2)}) copy-start(bf16[2,256,512]{2,1,0:T(8,128)(2,1)S(1)} %pad_maximum_fusion.refs_0_) | copy-start | bytes 1572868
  10.3 59.7 %collective-permute-start.3 = (bf16[2,256,512]{2,1,0:T(8,128)(2,1)S(1)}, bf16[2,256,512]{2,1,0:T(8,128)(2,1)S(1)}, u32[]{:S(2)}, u32[]{:S(2)}) collective-permute-start(bf16[2,256,512]{2,1,0:T(8,128)(2,1)S(1)} %pad_maximum_fusion.refs_0_), channel_id=1, source_target_pairs={{0,16},{16,0},{32,48},{48,32},{64,80},{80,64},{96,112},{112,96},{1... | collective-permute-start | bytes 1572872 | tf_op jit(solution)/shard_map/ppermute | solution.py:317
  10.4 37.6 %collective-permute-start.2 = (bf16[2,256,512]{2,1,0:T(8,128)(2,1)S(1)}, bf16[2,256,512]{2,1,0:T(8,128)(2,1)S(1)}, u32[]{:S(2)}, u32[]{:S(2)}) collective-permute-start(bf16[2,256,512]{2,1,0:T(8,128)(2,1)S(1)} %pad_maximum_fusion.refs_0_), channel_id=1, source_target_pairs={{0,96},{16,112},{32,0},{48,16},{64,32},{80,48},{96,64},{112,80},{1... | collective-permute-start | bytes 1572872 | tf_op jit(solution)/shard_map/ppermute | solution.py:314
  10.6 37.5 %collective-permute-start.1 = (bf16[2,256,512]{2,1,0:T(8,128)(2,1)S(1)}, bf16[2,256,512]{2,1,0:T(8,128)(2,1)}, u32[]{:S(2)}, u32[]{:S(2)}) collective-permute-start(bf16[2,256,512]{2,1,0:T(8,128)(2,1)S(1)} %pad_maximum_fusion.refs_0_), channel_id=1, source_target_pairs={{0,64},{16,80},{32,96},{48,112},{64,0},{80,16},{96,32},{112,48},{1... | collective-permute-start | bytes 1572872 | tf_op jit(solution)/shard_map/ppermute | solution.py:314
  13.9 34.7 %collective-permute-start = (bf16[2,256,512]{2,1,0:T(8,128)(2,1)S(1)}, bf16[2,256,512]{2,1,0:T(8,128)(2,1)}, u32[]{:S(2)}, u32[]{:S(2)}) collective-permute-start(bf16[2,256,512]{2,1,0:T(8,128)(2,1)S(1)} %pad_maximum_fusion.refs_0_), channel_id=1, source_target_pairs={{0,32},{16,48},{32,64},{48,80},{64,96},{80,112},{96,0},{112,16},{1... | collective-permute-start | bytes 1572872 | tf_op jit(solution)/shard_map/ppermute | solution.py:314
  26.9 1.0 copy-start
  40.3 21.0 %all-to-all-start.2 = ((bf16[16,144,128]{2,1,0:T(8,128)(2,1)}), bf16[16,144,128]{2,1,0:T(8,128)(2,1)S(1)}, u32[]{:S(2)}, u32[]{:S(2)}) async-start(bf16[16,144,128]{2,1,0:T(8,128)(2,1)} %prefix0.1), calls=%async_computation.2 | async-start | bytes 1179648 | tf_op jit(solution)/shard_map/all_to_all | solution.py:352
  48.0 13.3 %copy-start.5 = (bf16[2,256,512]{2,1,0:T(8,128)(2,1)}, bf16[2,256,512]{2,1,0:T(8,128)(2,1)S(1)}, u32[]{:S(2)}) copy-start(bf16[2,256,512]{2,1,0:T(8,128)(2,1)S(1)} %collective-permute-done.2.refs_3_) | copy-start | bytes 1572868
  48.0 22.0 %collective-permute-start.6 = (bf16[2,256,512]{2,1,0:T(8,128)(2,1)S(1)}, bf16[2,256,512]{2,1,0:T(8,128)(2,1)}, u32[]{:S(2)}, u32[]{:S(2)}) collective-permute-start(bf16[2,256,512]{2,1,0:T(8,128)(2,1)S(1)} %collective-permute-done.2.refs_3_), channel_id=1, source_target_pairs={{0,16},{16,0},{32,48},{48,32},{64,80},{80,64},{96,112},{112,96},{1... | collective-permute-start | bytes 1572872 | tf_op jit(solution)/shard_map/ppermute | solution.py:317
  48.1 21.9 %collective-permute-start.5 = (bf16[2,256,512]{2,1,0:T(8,128)(2,1)}, bf16[2,256,512]{2,1,0:T(8,128)(2,1)}, u32[]{:S(2)}, u32[]{:S(2)}) collective-permute-start(bf16[2,256,512]{2,1,0:T(8,128)(2,1)} %collective-permute-done.1.refs_2_), channel_id=1, source_target_pairs={{0,16},{16,0},{32,48},{48,32},{64,80},{80,64},{96,112},{112,96},{1... | collective-permute-start | bytes 1572872 | tf_op jit(solution)/shard_map/ppermute | solution.py:317
  48.6 21.4 %collective-permute-start.4 = (bf16[2,256,512]{2,1,0:T(8,128)(2,1)}, bf16[2,256,512]{2,1,0:T(8,128)(2,1)}, u32[]{:S(2)}, u32[]{:S(2)}) collective-permute-start(bf16[2,256,512]{2,1,0:T(8,128)(2,1)} %collective-permute-done.refs_1_), channel_id=1, source_target_pairs={{0,16},{16,0},{32,48},{48,32},{64,80},{80,64},{96,112},{112,96},{1... | collective-permute-start | bytes 1572872 | tf_op jit(solution)/shard_map/ppermute | solution.py:317
  61.3 8.7 %copy-start.2 = (bf16[16,144,128]{2,1,0:T(8,128)(2,1)}, bf16[16,144,128]{2,1,0:T(8,128)(2,1)S(1)}, u32[]{:S(2)}) copy-start(bf16[16,144,128]{2,1,0:T(8,128)(2,1)S(1)} %all-to-all-done.2.r_ref) | copy-start | bytes 1769476
  61.4 19.8 %all-to-all-start.1 = ((bf16[16,144,128]{2,1,0:T(8,128)(2,1)}), bf16[16,144,128]{2,1,0:T(8,128)(2,1)S(1)}, u32[]{:S(2)}, u32[]{:S(2)}) async-start(bf16[16,144,128]{2,1,0:T(8,128)(2,1)} %prefix1.1), calls=%async_computation.1 | async-start | bytes 1179648 | tf_op jit(solution)/shard_map/all_to_all | solution.py:352
  70.0 0.8 copy-start.4
  81.2 0.8 copy-start.3

commit v2 on v0

v2 whole, which is shorter than its diff:
```python
import jax
import jax.numpy as jnp
import numpy as np
from jax import lax
from jax.experimental import pallas as pl
from jax.experimental.pallas import tpu as pltpu
from jax.sharding import PartitionSpec as P

HEADS = 64
KVH = 4
HD = 128
PROMPTS = 4
SAMP = 16
DEST = 16
T_LOCAL = 2048
CONT = 512
D = 4096
ROWS = 288
TAIL_PITCH = 1024
LOG2E = float(np.log2(np.e))
SCALE2 = float(np.log2(np.e) / np.sqrt(HD))
BF = jnp.bfloat16
F32 = jnp.float32
VMEM = pl.BlockSpec(memory_space=pltpu.VMEM)
SMEM = pl.BlockSpec(memory_space=pltpu.SMEM)
ANY = pl.BlockSpec(memory_space=pl.ANY)
PARAMS = pltpu.CompilerParams(vmem_limit_bytes=60 * 2**20)


def dot(a, b):
    return jnp.dot(a, b, preferred_element_type=F32)


def dot_t(a, b):
    return lax.dot_general(a, b, (((1,), (1,)), ((), ())), preferred_element_type=F32)


def split3(x):
    hi = x.astype(BF).astype(F32)
    mid = (x - hi).astype(BF).astype(F32)
    return hi, mid, x - hi - mid


def iota(shape, dim):
    return lax.broadcasted_iota(jnp.int32, shape, dim)


def one_hot(mask):
    return jnp.where(mask, 1.0, 0.0).astype(BF)


def cont_kernel(
    len_ref, prompt_ref, q_ref, k_hbm, v_hbm, tail_hbm, pm_ref, un_ref, kb, vb, sb, wb, ob, tail_ref, sem, tsem
):
    loads = [pltpu.make_async_copy(k_hbm.at[s], kb.at[s], sem.at[s]) for s in range(4)]
    loads += [pltpu.make_async_copy(v_hbm.at[s], vb.at[s], sem.at[4 + s]) for s in range(4)]
    for load in loads:
        load.start()

    row, col = iota((64, 64), 0), iota((64, 64), 1)
    prompt = jnp.broadcast_to(prompt_ref[...].astype(F32), (64, 64))
    prompt_col = jnp.where(row == col, prompt, 0.0).sum(1, keepdims=True)
    before = jnp.where((prompt == prompt_col) & (col < row), 1.0, 0.0).sum(1, keepdims=True)
    place = prompt_col * SAMP + before
    here = jnp.broadcast_to(place, (64, 64)) == col.astype(F32)
    un_ref[...] = one_hot(here)
    place_row = jnp.where(row == col, jnp.broadcast_to(place, (64, 64)), 0.0).sum(0, keepdims=True)
    c64, r64 = iota((64, 256), 1), iota((64, 256), 0)
    pick = one_hot(r64 == 4 * (c64 >> 4) + (c64 & 3))
    place_c = dot(jnp.broadcast_to(place_row, (8, 64)).astype(BF), pick)[:1]
    r, c = iota((256, 256), 0), iota((256, 256), 1)
    wanted = ((r >> 6) * SAMP + (r & 15)).astype(F32)
    pm_ref[...] = one_hot(
        (jnp.broadcast_to(place_c, (256, 256)) == wanted) & (((r >> 4) & 3) == ((c >> 2) & 3))
    )

    for s in range(4):
        loads[s].wait()
        live = iota((64, CONT), 1) < len_ref[s]
        for k in range(KVH):
            at = 64 * s + 16 * k
            sb[at : at + 16] = dot_t(q_ref[at : at + 16], kb[s, k])
        sb[64 * s : 64 * s + 64] = jnp.where(live, sb[64 * s : 64 * s + 64], -jnp.inf)
    logit = sb[...]
    top = logit.max(1, keepdims=True)
    w = jnp.exp2((logit - top) * SCALE2)
    total = w.sum(1, keepdims=True)
    wb[...] = w.astype(BF)
    for s in range(4):
        loads[4 + s].wait()
        for k in range(KVH):
            at = 64 * s + 16 * k
            ob[at : at + 16] = dot(wb[at : at + 16], vb[s, k])
    o = ob[...] * (1.0 / total)
    lane = iota((256, 128), 1)
    terms = jnp.zeros((256, 128), F32)
    for n, part in enumerate(split3(top * SCALE2 + jnp.log(total) * LOG2E)):
        terms = terms + jnp.where(lane == n, jnp.broadcast_to(part, (256, 128)), 0.0)
    turn = one_hot(c == (r & 3) * 64 + (r >> 2))
    moved = dot(turn, jnp.concatenate([o, terms], 1).astype(BF))
    tail_ref[:, 16:32, :] = jnp.zeros((DEST, 16, 128), F32)
    tail_ref[:, :16, :] = moved[:, :128].reshape(DEST, 16, 128)
    r16 = iota((256, 128), 0) & 15
    for n in range(3):
        term = jnp.broadcast_to(moved[:, 128 + n : 129 + n], (256, 128))
        tail_ref[:, 22 + n, :] = jnp.where(lane == r16, term, 0.0).reshape(DEST, 16, 128).sum(1)
    send = pltpu.make_async_copy(tail_ref, tail_hbm.at[:, 0:32], tsem)
    send.start()
    send.wait()


def cont_call(lengths, prompt, q_rows, keys, values):
    return pl.pallas_call(
        cont_kernel,
        out_shape=(
            jax.ShapeDtypeStruct((DEST, TAIL_PITCH, 128), F32),
            jax.ShapeDtypeStruct((256, 256), BF),
            jax.ShapeDtypeStruct((64, 64), BF),
        ),
        in_specs=[SMEM, VMEM, VMEM, ANY, ANY],
        out_specs=(ANY, VMEM, VMEM),
        scratch_shapes=[
            pltpu.VMEM((4, KVH, CONT, HD), BF),
            pltpu.VMEM((4, KVH, CONT, HD), BF),
            pltpu.VMEM((256, CONT), F32),
            pltpu.VMEM((256, CONT), BF),
            pltpu.VMEM((256, HD), F32),
            pltpu.VMEM((DEST, 32, 128), F32),
            pltpu.SemaphoreType.DMA((8,)),
            pltpu.SemaphoreType.DMA,
        ],
        compiler_params=PARAMS,
        cost_estimate=pl.CostEstimate(flops=2 * 10**9, bytes_accessed=2**22, transcendentals=131072),
        name="cont",
    )(lengths, prompt, q_rows, keys, values)


NB = KVH * PROMPTS
TC = 512


GROUPS = ((0, 1), (1, 3), (3, 6), (6, 10), (10, 16))
AHEAD = 2


def prefix_kernel(
    prompt, qv, tail_hbm, k_hbm, v_hbm, o_hbm, qs, kb, vb, sbuf, st, tv, ov, order, seen, tsem, ks, vs, osem
):
    loads = []
    for b in range(NB):
        k, p = b // PROMPTS, b % PROMPTS
        loads.append(
            (
                pltpu.make_async_copy(k_hbm.at[p, k], kb.at[b], ks.at[b]),
                pltpu.make_async_copy(v_hbm.at[p, k], vb.at[b], vs.at[b]),
            )
        )
    load_tail = pltpu.make_async_copy(tail_hbm.at[:, 0:32], tv, tsem)

    def start(group):
        for b in range(*GROUPS[group]):
            for load in loads[b]:
                load.start()
        if group == 1:
            load_tail.start()

    for group in range(AHEAD):
        start(group)
    r, c = iota((256, 256), 0), iota((256, 256), 1)
    turn = one_hot(c == (r & 15) * 16 + (r >> 4))

    def gather(k):
        for p in range(PROMPTS):
            b = k * PROMPTS + p
            for i in range(SAMP):
                qs[b, 16 * i : 16 * i + 16] = qv[order[16 * p + i], k]
            qs[b] = dot(turn, qs[b]).astype(BF)

    row = iota((256, 128), 0) & 63
    lane = iota((256, 128), 1)
    spot = iota((4, 16, 128), 1)
    sends = []

    def finish(b, o, top, total):
        k, p = b // PROMPTS, b % PROMPTS
        at = slice(4 * k, 4 * k + 4)
        o = (o * (1.0 / total)).astype(BF)
        ov[at, 64 * p : 64 * p + 64, :] = o.reshape(4, 64, 128)
        lse = top * SCALE2 + jnp.log(total) * LOG2E
        part = jnp.where(lane == (p % 2) * 64 + row, jnp.broadcast_to(lse, (256, 128)), 0.0)
        part = part.reshape(4, 64, 128).sum(1)
        st[p // 2, k] = part if p % 2 == 0 else st[p // 2, k] + part
        if p == PROMPTS - 1:
            ov[at, 256:272, :] = tv[at, :16].astype(BF)
            tail = tv[at, 16:32]
            for half in range(2):
                for n, part in enumerate(split3(st[half, k])):
                    tail = jnp.where(spot == 2 * n + half, part[:, None, :], tail)
            ov[at, 272:288, :] = tail.astype(BF)
            send = pltpu.make_async_copy(ov.at[at], o_hbm.at[at], osem.at[k])
            send.start()
            sends.append(send)

    for p in range(PROMPTS):
        seen[p] = 0

    def place(n, carry):
        p = prompt[0, n]
        rank = seen[p]
        order[p * SAMP + rank] = n
        seen[p] = rank + 1
        return carry

    lax.fori_loop(0, 64, place, 0, unroll=8)
    gather(0)
    prev_top = None
    for b in range(NB + 1):
        peak = None
        if b < NB:
            if b == 3:
                load_tail.wait()
            for group, (first, last) in enumerate(GROUPS):
                if b == first:
                    for member in range(first, last):
                        for load in loads[member]:
                            load.wait()
                    if group + AHEAD < len(GROUPS):
                        start(group + AHEAD)
            if b in (3, 6, 10):
                gather({3: 1, 6: 2, 10: 3}[b])
            q = qs[b]
        if b > 0:
            acc = total = None
        for t in range(T_LOCAL // TC):
            cols = slice(t * TC, (t + 1) * TC)
            if b < NB:
                s = dot_t(q, kb[b, cols])
                sbuf[b % 2, :, cols] = s
                for z in range(TC // 128):
                    piece = s[:, 128 * z : 128 * z + 128]
                    peak = piece if peak is None else jnp.maximum(peak, piece)
            if b > 0:
                w = jnp.exp2((sbuf[(b - 1) % 2, :, cols] - prev_top) * SCALE2)
                for z in range(TC // 128):
                    piece = w[:, 128 * z : 128 * z + 128]
                    total = piece if total is None else total + piece
                o = dot(w.astype(BF), vb[b - 1, cols])
                acc = o if acc is None else acc + o
        if b > 0:
            finish(b - 1, acc, prev_top, total.sum(1, keepdims=True))
        if b < NB:
            prev_top = peak.max(1, keepdims=True)
    for send in sends:
        send.wait()


def prefix_call(prompt, q, tail, keys, values):
    return pl.pallas_call(
        prefix_kernel,
        out_shape=jax.ShapeDtypeStruct((DEST, ROWS, 128), BF),
        in_specs=[SMEM, VMEM, ANY, ANY, ANY],
        out_specs=ANY,
        scratch_shapes=[
            pltpu.VMEM((NB, 256, 128), BF),
            pltpu.VMEM((NB, T_LOCAL, HD), BF),
            pltpu.VMEM((NB, T_LOCAL, HD), BF),
            pltpu.VMEM((2, 256, T_LOCAL), F32),
            pltpu.VMEM((2, KVH, 4, 128), F32),
            pltpu.VMEM((DEST, 32, 128), F32),
            pltpu.VMEM((DEST, ROWS, 128), BF),
            pltpu.SMEM((64,), jnp.int32),
            pltpu.SMEM((PROMPTS,), jnp.int32),
            pltpu.SemaphoreType.DMA,
            pltpu.SemaphoreType.DMA((NB,)),
            pltpu.SemaphoreType.DMA((NB,)),
            pltpu.SemaphoreType.DMA((KVH,)),
        ],
        compiler_params=pltpu.CompilerParams(vmem_limit_bytes=50 * 2**20),
        cost_estimate=pl.CostEstimate(flops=9 * 10**9, bytes_accessed=18 * 2**20, transcendentals=2**23),
        name="prefix",
    )(prompt, q, tail, keys, values)


def pack_kernel(*refs):
    w_hbm, out_ref, sem = refs[:8], refs[8], refs[9]
    loads = [pltpu.make_async_copy(w_hbm[n], out_ref.at[n], sem.at[n]) for n in range(8)]
    for load in loads:
        load.start()
    for load in loads:
        load.wait()


def pack_call(weights):
    return pl.pallas_call(
        pack_kernel,
        out_shape=jax.ShapeDtypeStruct((8, 512, 512), BF),
        in_specs=[ANY] * 8,
        out_specs=ANY,
        scratch_shapes=[pltpu.SemaphoreType.DMA((8,))],
        compiler_params=pltpu.CompilerParams(vmem_limit_bytes=16 * 2**20),
        cost_estimate=pl.CostEstimate(flops=0, bytes_accessed=8 * 2**20, transcendentals=0),
        name="pack",
    )(*weights)


def project_kernel(r_ref, pm_ref, un_ref, w_hbm, z_ref, wv, yv, zf, wsem):
    loads = [pltpu.make_async_copy(w_hbm.at[n], wv.at[n], wsem.at[n]) for n in range(8)]
    for load in loads:
        load.start()
    f = lambda x: x.astype(F32)
    lane = iota((256, 128), 1)
    row = iota((256, 128), 0)
    pad = jnp.zeros((112, 128), F32)
    logs = []
    for half in range(2):
        part = f(r_ref[:, 272 + half]) + f(r_ref[:, 274 + half]) + f(r_ref[:, 276 + half])
        logs.append(jnp.transpose(jnp.concatenate([part, pad], 0)))
    logs = jnp.concatenate(logs, 0)
    cont = r_ref[:, 256:272].reshape(256, 128)
    terms = jnp.zeros((256, 128), F32)
    for n in range(3):
        term = jnp.broadcast_to(f(r_ref[:, 278 + n])[:, None, :], (16, 16, 128)).reshape(256, 128)
        term = jnp.where(lane == (row & 15), term, 0.0).sum(1, keepdims=True)
        terms = terms + jnp.where(lane == n, jnp.broadcast_to(term, (256, 128)), 0.0)
    moved = dot(pm_ref[...], jnp.concatenate([cont, terms.astype(BF)], 1))
    log_c = moved[:, 128:129] + moved[:, 129:130] + moved[:, 130:131]
    top = jnp.maximum(jnp.where(lane < 16, logs, -jnp.inf).max(1, keepdims=True), log_c)
    w_c = jnp.exp2(log_c - top)
    w_p = jnp.exp2(jnp.where(lane < 16, logs - top, -jnp.inf))
    den = w_p.sum(1, keepdims=True) + w_c
    num = w_c * moved[:, :128]
    for src in range(16):
        num = num + w_p[:, src : src + 1] * f(r_ref[src, :256])
    mixed = (num / den).astype(BF).reshape(4, 4, 16, 128)
    mixed = jnp.concatenate([mixed[:, jj].reshape(64, 128) for jj in range(4)], 1)
    mixed = dot(un_ref[...], mixed).astype(BF)
    member = lax.axis_index("group")
    z, core = member >> 1, member & 1
    for load in loads:
        load.wait()
    for n in range(8):
        g = 2 * ((z - n % 4) & 3) + (core if n < 4 else 1 - core)
        yv[g] = dot(mixed, wv[n])
    for g in range(8):
        cols = slice(512 * (g % 2), 512 * (g % 2) + 512)
        zf[:, 4 * (g // 2) : 4 * (g // 2) + 4, cols] = yv[g].reshape(DEST, 4, 512)
    z_ref[...] = zf[...].astype(BF)


def project_call(received, pm, unsort, weights):
    return pl.pallas_call(
        project_kernel,
        out_shape=jax.ShapeDtypeStruct((DEST, 16, 1024), BF),
        in_specs=[VMEM] * 3 + [ANY],
        out_specs=VMEM,
        scratch_shapes=[
            pltpu.VMEM((8, 512, 512), BF),
            pltpu.VMEM((8, 64, 512), F32),
            pltpu.VMEM((DEST, 16, 1024), F32),
            pltpu.SemaphoreType.DMA((8,)),
        ],
        compiler_params=pltpu.CompilerParams(vmem_limit_bytes=52 * 2**20),
        cost_estimate=pl.CostEstimate(flops=3 * 10**8, bytes_accessed=4 * 2**20, transcendentals=2**15),
        name="project",
    )(received, pm, unsort, weights)


def sum_kernel(r_ref, o_ref):
    total = r_ref[0].astype(F32)
    for src in range(1, DEST):
        total = total + r_ref[src].astype(F32)
    for quarter in range(4):
        o_ref[0, :, 1024 * quarter : 1024 * quarter + 1024] = total[
            4 * quarter : 4 * quarter + 4
        ].astype(BF)


def sum_call(received):
    return pl.pallas_call(
        sum_kernel,
        out_shape=jax.ShapeDtypeStruct((1, 4, D), BF),
        in_specs=[VMEM],
        out_specs=VMEM,
        compiler_params=pltpu.CompilerParams(vmem_limit_bytes=16 * 2**20),
        name="sum",
    )(received)


def gather_weights(w_out, seq):
    own = lax.optimization_barrier(lax.dynamic_slice_in_dim(w_out, 4 * seq * HD, 4 * HD, 0))
    blocks = [own]
    for k in (1, 2, 3):
        hop = [(2 * a + c, 2 * ((a + k) % 4) + c) for a in range(4) for c in range(2)]
        blocks.append(lax.ppermute(own, "group", hop))
    return blocks


def per_device(
    queries, prefix_keys, prefix_values, cont_keys, cont_values, cont_len, prompt_of, w_out
):
    q_rows = queries.reshape(4 * HEADS, HD)
    copies = jnp.broadcast_to(q_rows[None], (DEST, 4 * HEADS, HD))
    copies, w_out = lax.optimization_barrier((copies, w_out))
    gathered = lax.all_to_all(copies, "seq", 0, 0).reshape(64, KVH, 16, HD)
    weights = gather_weights(w_out, lax.axis_index("seq"))
    tail, pm, unsort = cont_call(cont_len[0], prompt_of, q_rows, cont_keys[0], cont_values[0])
    part = prefix_call(prompt_of, gathered, tail, prefix_keys[0], prefix_values[0])
    part, weights = lax.optimization_barrier((part, weights))
    swap = [(j, j ^ 1) for j in range(8)]
    weights = weights + [lax.ppermute(b, "group", swap) for b in weights]
    received = lax.all_to_all(part, "seq", 0, 0)
    y = project_call(received, pm, unsort, pack_call(weights))
    return sum_call(lax.all_to_all(y, "seq", 0, 0))


def solution(mesh):
    return jax.shard_map(
        per_device,
        mesh=mesh,
        in_specs=(
            P("group", "seq", None),
            P("group", None, None, "seq", None),
            P("group", None, None, "seq", None),
            P("group", "seq", None, None, None),
            P("group", "seq", None, None, None),
            P("group", "seq"),
            P("group", None),
            P(None, "group"),
        ),
        out_specs=P("group", "seq", None),
        check_vma=False,
    )
```

time: 306 us -> 82.5 us (0.27)
  blocking collectives: 163 us -> 13.7 us
  matrix products: 41.6 us -> 0 us
  Pallas kernels: 0 us -> 26.7 us
  waiting for transfers between devices: 43.3 us -> 18.5 us
  other arithmetic: 22.8 us -> 0 us
  starting transfers between devices: 0.04 us -> 17.6 us
  between operations: 14.2 us -> 0.14 us
  local copies, waits for them, and re-layouts: 18 us -> 5.26 us
    pmax x1 -> x0, blocking collectives: 72.1 us -> none  [per_device(): highest = lax.pmax(pre_peak, 'seq')]
    unnamed x1 -> x0, blocking collectives: 69.8 us -> none
    all_gather x1 -> x0, waiting for transfers between devices: 43.2 us -> none  [per_device(): gathered = lax.all_gather(queries, 'seq', axis=1, tiled=True)[0]]
    dot_general x5 -> x0, matrix products: 41.6 us -> none  [the longest x1 17.5 us: per_device(): jnp.einsum('pskjt,pktd->pskjd', weights.astype(jnp.bfloat16), prefix_valu...]
    pallas_call x0 -> x5, Pallas kernels: none -> 26.7 us  [the longest x1 15.5 us: prefix_call(): pl.pallas_call(prefix_kernel, out_shape=jax.ShapeDtypeStruct((DEST, ROWS,...]
    all_to_all x0 -> x2, waiting for transfers between devices: none -> 15.4 us  [the longest x1 10.1 us: per_device(): received = lax.all_to_all(part, 'seq', 0, 0)]
    reduce_sum x2 -> x0, other arithmetic: 14.3 us -> none  [the longest x1 14 us: per_device(): totals = weights.sum(-1)]
    all_gather x1 -> x0, blocking collectives: 13.3 us -> none  [per_device(): lax.all_gather(mixed, 'group', axis=0, tiled=True)]
  transfers between devices with their start and end apart: 2 -> 9, of which waited for: 1 -> 6; matrix products, arithmetic and copies ran while one was open for 3% -> 1% of each run, Pallas kernels for 0% -> 26%
where the time goes in v2:
time: 82.5 us; the launch traced here: 82 us
  Pallas kernels  26.7 us (32%)
  waiting for transfers between devices  18.5 us (22%)
  starting transfers between devices  17.6 us (21%)
  blocking collectives  13.7 us (17%)
  local copies, waits for them, and re-layouts  5.26 us (6%)
    pallas_call x1, Pallas kernels, prefix_call(): pl.pallas_call(prefix_kernel, out_shape=jax.ShapeDtypeStruct((DEST, ROWS,...  15.5 us
    all_to_all x1, blocking collectives, per_device(): return sum_call(lax.all_to_all(y, 'seq', 0, 0))  13.7 us
    all_to_all x1, waiting for transfers between devices, per_device(): received = lax.all_to_all(part, 'seq', 0, 0)  10.1 us
    all_to_all x1, starting transfers between devices, per_device(): gathered = lax.all_to_all(copies, 'seq', 0, 0).reshape(64, KVH, 16, HD)  7.03 us
    ppermute x3, starting transfers between devices, gather_weights(): blocks.append(lax.ppermute(own, 'group', hop))  5.68 us
    pallas_call x1, Pallas kernels, cont_call(): pl.pallas_call(cont_kernel, out_shape=(jax.ShapeDtypeStruct((DEST, TAIL_P...  5.68 us
    all_to_all x1, waiting for transfers between devices, per_device(): gathered = lax.all_to_all(copies, 'seq', 0, 0).reshape(64, KVH, 16, HD)  5.24 us
    pallas_call x1, Pallas kernels, project_call(): pl.pallas_call(project_kernel, out_shape=jax.ShapeDtypeStruct((DEST, 16,...  4.42 us
  transfers between devices with their start and end apart: 9, of which 6 were waited for; matrix products, arithmetic and copies ran while one was open for 1% of the time, Pallas kernels for 26%

profile of v2, /device:TPU:32, one launch (start us, length us, event | category | flops | bytes accessed | tf_op | source)
XLA Modules:
  0.0 82.0 jit_solution(18047481634252926782)
XLA Ops:
  0.0 0.0 copy-start.3
  0.0 0.9 %broadcast_in_dim.7.q_ref = bf16[256,128]{1,0:T(8,128)(2,1)S(1)} reshape(bf16[1,4,8192]{2,1,0:T(4,128)(2,1)} %param.8) | data formatting | bytes 131072 | tf_op jit(solution)/shard_map/broadcast_in_dim | solution.py:402
  0.9 0.0 copy-start.4
  1.0 1.3 %broadcast_in_dim.8 = bf16[16,256,128]{2,1,0:T(8,128)(2,1)} broadcast(bf16[256,128]{1,0:T(8,128)(2,1)S(1)} %broadcast_in_dim.7.q_ref), dimensions={1,2} | broadcast | bytes 1114112 | tf_op jit(solution)/shard_map/broadcast_in_dim | solution.py:402
  2.2 7.0 %all-to-all-start = ((bf16[16,256,128]{2,1,0:T(8,128)(2,1)}), bf16[16,256,128]{2,1,0:T(8,128)(2,1)S(1)}, u32[]{:S(2)}, u32[]{:S(2)}) async-start(bf16[16,256,128]{2,1,0:T(8,128)(2,1)} %broadcast_in_dim.8), calls=%async_computation | async-start | bytes 2097152 | tf_op jit(solution)/shard_map/all_to_all | solution.py:404
  9.3 1.1 %constant_dynamic-slice_fusion.refs_0_ = bf16[512,512]{1,0:T(8,128)(2,1)S(1)} fusion(bf16[8192,512]{1,0:T(8,128)(2,1)} %param.15, s32[]{:T(128)S(6)} %select_n.3), kind=kLoop, calls=%fused_computation | loop fusion | bytes 1048580 | tf_op jit(solution)/shard_map/dynamic_slice | solution.py:390
  10.4 2.0 %collective-permute-start = (bf16[512,512]{1,0:T(8,128)(2,1)S(1)}, bf16[512,512]{1,0:T(8,128)(2,1)S(1)}, u32[]{:S(2)}, u32[]{:S(2)}) collective-permute-start(bf16[512,512]{1,0:T(8,128)(2,1)S(1)} %constant_dynamic-slice_fusion.refs_0_), channel_id=1, source_target_pairs={{0,32},{16,48},{32,64},{48,80},{64,96},{80,112},{96,0},{112,16},{1... | collective-permute-start | bytes 1572872 | tf_op jit(solution)/shard_map/ppermute | solution.py:394
  12.3 1.2 %collective-permute-start.1 = (bf16[512,512]{1,0:T(8,128)(2,1)S(1)}, bf16[512,512]{1,0:T(8,128)(2,1)S(1)}, u32[]{:S(2)}, u32[]{:S(2)}) collective-permute-start(bf16[512,512]{1,0:T(8,128)(2,1)S(1)} %constant_dynamic-slice_fusion.refs_0_), channel_id=1, source_target_pairs={{0,64},{16,80},{32,96},{48,112},{64,0},{80,16},{96,32},{112,48},{1... | collective-permute-start | bytes 1572872 | tf_op jit(solution)/shard_map/ppermute | solution.py:394
  13.5 2.5 %collective-permute-start.2 = (bf16[512,512]{1,0:T(8,128)(2,1)S(1)}, bf16[512,512]{1,0:T(8,128)(2,1)S(1)}, u32[]{:S(2)}, u32[]{:S(2)}) collective-permute-start(bf16[512,512]{1,0:T(8,128)(2,1)S(1)} %constant_dynamic-slice_fusion.refs_0_), channel_id=1, source_target_pairs={{0,96},{16,112},{32,0},{48,16},{64,32},{80,48},{96,64},{112,80},{1... | collective-permute-start | bytes 1572872 | tf_op jit(solution)/shard_map/ppermute | solution.py:394
  16.0 0.0 copy-done.4
  16.0 5.7 %cont.1 = (f32[16,1024,128]{2,1,0:T(8,128)}, bf16[256,256]{1,0:T(8,128)(2,1)}, bf16[64,64]{1,0:T(8,128)(2,1)}) custom-call(s32[4]{0:T(128)} %bitcast.11, s32[1,64]{1,0:T(1,128)} %prompt.1, bf16[256,128]{1,0:T(8,128)(2,1)} %copy-done.4, bf16[4,4,512,128]{3,2,1,0:T(8,128)(2,1)} %bitcast.9, bf16[4,4,512,128]{3,2,1,0:T(8,128)(2,1)} %bitcast.10), custom_call_target="tpu_custom_call" | custom-call | flops 2000000000 | bytes 4194304 | tf_op jit(solution)/shard_map/cont/pallas_call | solution.py:113
  21.7 5.2 %all-to-all-done = bf16[16,256,128]{2,1,0:T(8,128)(2,1)S(1)} async-done(((bf16[16,256,128]{2,1,0:T(8,128)(2,1)}), bf16[16,256,128]{2,1,0:T(8,128)(2,1)S(1)}, u32[]{:S(2)}, u32[]{:S(2)}) %all-to-all-start) | async-done | bytes 1048608 | tf_op jit(solution)/shard_map/all_to_all | solution.py:404
  27.0 0.0 copy-done.3
  27.0 15.5 %prefix.1 = bf16[16,288,128]{2,1,0:T(8,128)(2,1)} custom-call(s32[1,64]{1,0:T(1,128)S(1)} %copy-done.3, bf16[64,4,16,128]{3,2,1,0:T(8,128)(2,1)S(1)} %bitcast.6, f32[16,1024,128]{2,1,0:T(8,128)} %get-tuple-element.16.tail_hbm, bf16[4,4,2048,128]{3,2,1,0:T(8,128)(2,1)} %bitcast.7, bf16[4,4,2048,128]{3,2,1,0:T(8,128)(2,1)} %bitcast.8), custom_call_target="tpu_custom_call" | custom-call | flops 8999999488 | bytes 18874368 | tf_op jit(solution)/shard_map/prefix/pallas_call | solution.py:258
  42.5 0.0 copy-start.1
  42.5 0.0 copy-start.2
  42.5 0.0 collective-permute-done.refs_1_
  42.5 0.0 collective-permute-done.1.refs_2_
  42.5 0.0 collective-permute-done.2.refs_3_
  42.5 3.8 %all-to-all-start.1 = ((bf16[16,288,128]{2,1,0:T(8,128)(2,1)}), bf16[16,288,128]{2,1,0:T(8,128)(2,1)S(1)}, u32[]{:S(2)}, u32[]{:S(2)}) async-start(bf16[16,288,128]{2,1,0:T(8,128)(2,1)} %prefix.1), calls=%async_computation.1 | async-start | bytes 2359296 | tf_op jit(solution)/shard_map/all_to_all | solution.py:411
  46.4 0.1 collective-permute-start.3
  46.5 0.5 collective-permute-start.4
  47.0 0.1 collective-permute-start.5
  47.1 0.4 collective-permute-start.6
  47.5 0.9 %collective-permute-done.3.refs_4_ = bf16[512,512]{1,0:T(8,128)(2,1)S(1)} collective-permute-done((bf16[512,512]{1,0:T(8,128)(2,1)S(1)}, bf16[512,512]{1,0:T(8,128)(2,1)S(1)}, u32[]{:S(2)}, u32[]{:S(2)}) %collective-permute-start.3) | collective-permute-done | bytes 524320 | tf_op jit(solution)/shard_map/ppermute | solution.py:410
  48.4 0.7 collective-permute-done.4.refs_5_
  49.1 0.7 collective-permute-done.5.refs_6_
  49.9 0.7 collective-permute-done.6.refs_7_
  50.6 0.4 pack.1.w_hbm
  51.0 0.0 copy-start
  51.0 2.0 %copy-done = bf16[8,512,512]{2,1,0:T(8,128)(2,1)} copy-done((bf16[8,512,512]{2,1,0:T(8,128)(2,1)}, bf16[8,512,512]{2,1,0:T(8,128)(2,1)S(1)}, u32[]{:S(2)}) %copy-start) | copy-done | bytes 4194328
  53.0 10.1 %all-to-all-done.1.r_ref = bf16[16,288,128]{2,1,0:T(8,128)(2,1)S(1)} async-done(((bf16[16,288,128]{2,1,0:T(8,128)(2,1)}), bf16[16,288,128]{2,1,0:T(8,128)(2,1)S(1)}, u32[]{:S(2)}, u32[]{:S(2)}) %all-to-all-start.1) | async-done | bytes 1179680 | tf_op jit(solution)/shard_map/all_to_all | solution.py:411
  63.1 0.0 copy-done.1
  63.1 0.0 copy-done.2
  63.1 4.4 %project.1 = bf16[16,16,1024]{2,1,0:T(8,128)(2,1)S(1)} custom-call(bf16[16,288,128]{2,1,0:T(8,128)(2,1)S(1)} %all-to-all-done.1.r_ref, bf16[256,256]{1,0:T(8,128)(2,1)S(1)} %copy-done.1, bf16[64,64]{1,0:T(8,128)(2,1)S(1)} %copy-done.2, bf16[8,512,512]{2,1,0:T(8,128)(2,1)} %copy-done), custom_call_target="tpu_custom_call" | custom-call | flops 300000000 | bytes 4194304 | tf_op jit(solution)/shard_map/project/pallas_call | solution.py:351
  67.6 13.7 %all_to_all.15.r_ref = bf16[16,16,1024]{2,1,0:T(8,128)(2,1)S(1)} all-to-all(bf16[16,16,1024]{2,1,0:T(8,128)(2,1)S(1)} %project.1), channel_id=1, replica_groups=mesh['group'=8,'seq'=16] {'seq'}, dimensions={0} | all-to-all | bytes 1048576 | tf_op jit(solution)/shard_map/all_to_all | solution.py:413
  81.3 0.7 sum.1
Async XLA Ops:
  0.0 27.0 %copy-start.3 = (s32[1,64]{1,0:T(1,128)S(1)}, s32[1,64]{1,0:T(1,128)}, u32[]{:S(2)}) copy-start(s32[1,64]{1,0:T(1,128)} %prompt.1) | copy-start | bytes 772
  0.9 15.1 %copy-start.4 = (bf16[256,128]{1,0:T(8,128)(2,1)}, bf16[256,128]{1,0:T(8,128)(2,1)S(1)}, u32[]{:S(2)}) copy-start(bf16[256,128]{1,0:T(8,128)(2,1)S(1)} %broadcast_in_dim.7.q_ref) | copy-start | bytes 196612
  2.2 24.7 %all-to-all-start = ((bf16[16,256,128]{2,1,0:T(8,128)(2,1)}), bf16[16,256,128]{2,1,0:T(8,128)(2,1)S(1)}, u32[]{:S(2)}, u32[]{:S(2)}) async-start(bf16[16,256,128]{2,1,0:T(8,128)(2,1)} %broadcast_in_dim.8), calls=%async_computation | async-start | bytes 2097152 | tf_op jit(solution)/shard_map/all_to_all | solution.py:404
  10.4 32.2 %collective-permute-start = (bf16[512,512]{1,0:T(8,128)(2,1)S(1)}, bf16[512,512]{1,0:T(8,128)(2,1)S(1)}, u32[]{:S(2)}, u32[]{:S(2)}) collective-permute-start(bf16[512,512]{1,0:T(8,128)(2,1)S(1)} %constant_dynamic-slice_fusion.refs_0_), channel_id=1, source_target_pairs={{0,32},{16,48},{32,64},{48,80},{64,96},{80,112},{96,0},{112,16},{1... | collective-permute-start | bytes 1572872 | tf_op jit(solution)/shard_map/ppermute | solution.py:394
  12.3 30.2 %collective-permute-start.1 = (bf16[512,512]{1,0:T(8,128)(2,1)S(1)}, bf16[512,512]{1,0:T(8,128)(2,1)S(1)}, u32[]{:S(2)}, u32[]{:S(2)}) collective-permute-start(bf16[512,512]{1,0:T(8,128)(2,1)S(1)} %constant_dynamic-slice_fusion.refs_0_), channel_id=1, source_target_pairs={{0,64},{16,80},{32,96},{48,112},{64,0},{80,16},{96,32},{112,48},{1... | collective-permute-start | bytes 1572872 | tf_op jit(solution)/shard_map/ppermute | solution.py:394
  13.5 29.1 %collective-permute-start.2 = (bf16[512,512]{1,0:T(8,128)(2,1)S(1)}, bf16[512,512]{1,0:T(8,128)(2,1)S(1)}, u32[]{:S(2)}, u32[]{:S(2)}) collective-permute-start(bf16[512,512]{1,0:T(8,128)(2,1)S(1)} %constant_dynamic-slice_fusion.refs_0_), channel_id=1, source_target_pairs={{0,96},{16,112},{32,0},{48,16},{64,32},{80,48},{96,64},{112,80},{1... | collective-permute-start | bytes 1572872 | tf_op jit(solution)/shard_map/ppermute | solution.py:394
  42.5 20.6 %copy-start.1 = (bf16[256,256]{1,0:T(8,128)(2,1)S(1)}, bf16[256,256]{1,0:T(8,128)(2,1)}, u32[]{:S(2)}) copy-start(bf16[256,256]{1,0:T(8,128)(2,1)} %get-tuple-element.19.pm_ref) | copy-start | bytes 393220
  42.5 20.6 %copy-start.2 = (bf16[64,64]{1,0:T(8,128)(2,1)S(1)}, bf16[64,64]{1,0:T(8,128)(2,1)}, u32[]{:S(2)}) copy-start(bf16[64,64]{1,0:T(8,128)(2,1)} %get-tuple-element.20.un_ref) | copy-start | bytes 24580
  42.5 20.6 %all-to-all-start.1 = ((bf16[16,288,128]{2,1,0:T(8,128)(2,1)}), bf16[16,288,128]{2,1,0:T(8,128)(2,1)S(1)}, u32[]{:S(2)}, u32[]{:S(2)}) async-start(bf16[16,288,128]{2,1,0:T(8,128)(2,1)} %prefix.1), calls=%async_computation.1 | async-start | bytes 2359296 | tf_op jit(solution)/shard_map/all_to_all | solution.py:411
  46.4 2.0 %collective-permute-start.3 = (bf16[512,512]{1,0:T(8,128)(2,1)S(1)}, bf16[512,512]{1,0:T(8,128)(2,1)S(1)}, u32[]{:S(2)}, u32[]{:S(2)}) collective-permute-start(bf16[512,512]{1,0:T(8,128)(2,1)S(1)} %constant_dynamic-slice_fusion.refs_0_), channel_id=1, source_target_pairs={{0,16},{16,0},{32,48},{48,32},{64,80},{80,64},{96,112},{112,96},{1... | collective-permute-start | bytes 1572872 | tf_op jit(solution)/shard_map/ppermute | solution.py:410
  46.5 2.6 %collective-permute-start.4 = (bf16[512,512]{1,0:T(8,128)(2,1)S(1)}, bf16[512,512]{1,0:T(8,128)(2,1)S(1)}, u32[]{:S(2)}, u32[]{:S(2)}) collective-permute-start(bf16[512,512]{1,0:T(8,128)(2,1)S(1)} %collective-permute-done.refs_1_), channel_id=1, source_target_pairs={{0,16},{16,0},{32,48},{48,32},{64,80},{80,64},{96,112},{112,96},{1... | collective-permute-start | bytes 1572872 | tf_op jit(solution)/shard_map/ppermute | solution.py:410
  47.0 2.9 %collective-permute-start.5 = (bf16[512,512]{1,0:T(8,128)(2,1)S(1)}, bf16[512,512]{1,0:T(8,128)(2,1)S(1)}, u32[]{:S(2)}, u32[]{:S(2)}) collective-permute-start(bf16[512,512]{1,0:T(8,128)(2,1)S(1)} %collective-permute-done.1.refs_2_), channel_id=1, source_target_pairs={{0,16},{16,0},{32,48},{48,32},{64,80},{80,64},{96,112},{112,96},{1... | collective-permute-start | bytes 1572872 | tf_op jit(solution)/shard_map/ppermute | solution.py:410
  47.1 3.6 %collective-permute-start.6 = (bf16[512,512]{1,0:T(8,128)(2,1)S(1)}, bf16[512,512]{1,0:T(8,128)(2,1)S(1)}, u32[]{:S(2)}, u32[]{:S(2)}) collective-permute-start(bf16[512,512]{1,0:T(8,128)(2,1)S(1)} %collective-permute-done.2.refs_3_), channel_id=1, source_target_pairs={{0,16},{16,0},{32,48},{48,32},{64,80},{80,64},{96,112},{112,96},{1... | collective-permute-start | bytes 1572872 | tf_op jit(solution)/shard_map/ppermute | solution.py:410
  51.0 2.0 %copy-start = (bf16[8,512,512]{2,1,0:T(8,128)(2,1)}, bf16[8,512,512]{2,1,0:T(8,128)(2,1)S(1)}, u32[]{:S(2)}) copy-start(bf16[8,512,512]{2,1,0:T(8,128)(2,1)S(1)} %pack.1.w_hbm) | copy-start | bytes 12582916

commit v3 on v2

--- a/solution.py
+++ b/solution.py
@@ -49,22 +49,54 @@
     return jnp.where(mask, 1.0, 0.0).astype(BF)
 
 
+def copies_kernel(q_ref, out_hbm, sem):
+    sends = [pltpu.make_async_copy(q_ref.at[0], out_hbm.at[d], sem.at[d]) for d in range(DEST)]
+    for send in sends:
+        send.start()
+    for send in sends:
+        send.wait()
+
+
+def copies_call(queries):
+    return pl.pallas_call(
+        copies_kernel,
+        out_shape=jax.ShapeDtypeStruct((DEST, 4, HEADS * HD), BF),
+        in_specs=[VMEM],
+        out_specs=ANY,
+        scratch_shapes=[pltpu.SemaphoreType.DMA((DEST,))],
+        compiler_params=PARAMS,
+        name="copies",
+    )(queries)
+
+
+def place_of(prompt):
+    row, col = iota((64, 64), 0), iota((64, 64), 1)
+    prompt = jnp.broadcast_to(prompt.astype(F32), (64, 64))
+    prompt_col = jnp.where(row == col, prompt, 0.0).sum(1, keepdims=True)
+    before = jnp.where((prompt == prompt_col) & (col < row), 1.0, 0.0).sum(1, keepdims=True)
+    return jnp.broadcast_to(prompt_col * SAMP + before, (64, 64))
+
+
+def as_row(column):
+    row, col = iota((64, 64), 0), iota((64, 64), 1)
+    return jnp.where(row == col, column, 0.0).sum(0, keepdims=True)
+
+
 def cont_kernel(
-    len_ref, prompt_ref, q_ref, k_hbm, v_hbm, tail_hbm, pm_ref, un_ref, kb, vb, sb, wb, ob, tail_ref, sem, tsem
+    len_ref, prompt_ref, q_in, k_hbm, v_hbm, tail_hbm, pm_ref, un_ref, kb, vb, sb, wb, ob, tail_ref, qf, q_ref, sem, tsem
 ):
     loads = [pltpu.make_async_copy(k_hbm.at[s], kb.at[s], sem.at[s]) for s in range(4)]
     loads += [pltpu.make_async_copy(v_hbm.at[s], vb.at[s], sem.at[4 + s]) for s in range(4)]
     for load in loads:
         load.start()
 
-    row, col = iota((64, 64), 0), iota((64, 64), 1)
-    prompt = jnp.broadcast_to(prompt_ref[...].astype(F32), (64, 64))
-    prompt_col = jnp.where(row == col, prompt, 0.0).sum(1, keepdims=True)
-    before = jnp.where((prompt == prompt_col) & (col < row), 1.0, 0.0).sum(1, keepdims=True)
-    place = prompt_col * SAMP + before
-    here = jnp.broadcast_to(place, (64, 64)) == col.astype(F32)
-    un_ref[...] = one_hot(here)
-    place_row = jnp.where(row == col, jnp.broadcast_to(place, (64, 64)), 0.0).sum(0, keepdims=True)
+    for h in range(HEADS):
+        qf[pl.ds(h, 4, stride=HEADS), :] = q_in[0, :, HD * h : HD * h + HD].astype(F32)
+    q_ref[...] = qf[...].astype(BF)
+
+    place = place_of(prompt_ref[...])
+    un_ref[...] = one_hot(place == iota((64, 64), 1).astype(F32))
+    place_row = as_row(place)
     c64, r64 = iota((64, 256), 1), iota((64, 256), 0)
     pick = one_hot(r64 == 4 * (c64 >> 4) + (c64 & 3))
     place_c = dot(jnp.broadcast_to(place_row, (8, 64)).astype(BF), pick)[:1]
@@ -109,7 +141,7 @@
     send.wait()
 
 
-def cont_call(lengths, prompt, q_rows, keys, values):
+def cont_call(lengths, prompt, queries, keys, values):
     return pl.pallas_call(
         cont_kernel,
         out_shape=(
@@ -126,55 +158,59 @@
             pltpu.VMEM((256, CONT), BF),
             pltpu.VMEM((256, HD), F32),
             pltpu.VMEM((DEST, 32, 128), F32),
+            pltpu.VMEM((256, HD), F32),
+            pltpu.VMEM((256, HD), BF),
             pltpu.SemaphoreType.DMA((8,)),
             pltpu.SemaphoreType.DMA,
         ],
         compiler_params=PARAMS,
         cost_estimate=pl.CostEstimate(flops=2 * 10**9, bytes_accessed=2**22, transcendentals=131072),
         name="cont",
-    )(lengths, prompt, q_rows, keys, values)
+    )(lengths, prompt, queries, keys, values)
 
 
 NB = KVH * PROMPTS
 TC = 512
 
 
-GROUPS = ((0, 1), (1, 3), (3, 6), (6, 10), (10, 16))
+GROUPS = ((0, 2), (2, 6), (6, 16))
 AHEAD = 2
 
 
 def prefix_kernel(
-    prompt, qv, tail_hbm, k_hbm, v_hbm, o_hbm, qs, kb, vb, sbuf, st, tv, ov, order, seen, tsem, ks, vs, osem
+    prompt, q_ref, tail_hbm, k_hbm, v_hbm, o_hbm, qs, kb, vb, sbuf, st, tv, ov, qf, qb, tsem, ks, vs, osem
 ):
     loads = []
-    for b in range(NB):
-        k, p = b // PROMPTS, b % PROMPTS
-        loads.append(
-            (
-                pltpu.make_async_copy(k_hbm.at[p, k], kb.at[b], ks.at[b]),
-                pltpu.make_async_copy(v_hbm.at[p, k], vb.at[b], vs.at[b]),
-            )
-        )
+    for first, last in GROUPS:
+        loads.append([])
+        while first < last:
+            k, p = first // PROMPTS, first % PROMPTS
+            stop = min(last, (k + 1) * PROMPTS)
+            for hbm, buf, sem in ((k_hbm, kb, ks), (v_hbm, vb, vs)):
+                source = hbm.at[p : p + stop - first, k]
+                loads[-1].append(pltpu.make_async_copy(source, buf.at[first:stop], sem.at[first]))
+            first = stop
     load_tail = pltpu.make_async_copy(tail_hbm.at[:, 0:32], tv, tsem)
 
     def start(group):
-        for b in range(*GROUPS[group]):
-            for load in loads[b]:
-                load.start()
+        for load in loads[group]:
+            load.start()
         if group == 1:
             load_tail.start()
 
     for group in range(AHEAD):
         start(group)
-    r, c = iota((256, 256), 0), iota((256, 256), 1)
-    turn = one_hot(c == (r & 15) * 16 + (r >> 4))
+    sort = one_hot(as_row(place_of(prompt[...])) == iota((64, 64), 0).astype(F32))
+    for d in range(DEST):
+        qf[4 * d : 4 * d + 4, :] = q_ref[d].astype(F32)
+    qb[...] = qf[...].astype(BF)
 
     def gather(k):
+        ordered = dot(sort, qb[:, 2048 * k : 2048 * k + 2048]).astype(BF)
         for p in range(PROMPTS):
-            b = k * PROMPTS + p
-            for i in range(SAMP):
-                qs[b, 16 * i : 16 * i + 16] = qv[order[16 * p + i], k]
-            qs[b] = dot(turn, qs[b]).astype(BF)
+            for j in range(16):
+                piece = ordered[16 * p : 16 * p + 16, 128 * j : 128 * j + 128]
+                qs[k * PROMPTS + p, 16 * j : 16 * j + 16] = piece
 
     row = iota((256, 128), 0) & 63
     lane = iota((256, 128), 1)
@@ -201,33 +237,21 @@
             send.start()
             sends.append(send)
 
-    for p in range(PROMPTS):
-        seen[p] = 0
-
-    def place(n, carry):
-        p = prompt[0, n]
-        rank = seen[p]
-        order[p * SAMP + rank] = n
-        seen[p] = rank + 1
-        return carry
-
-    lax.fori_loop(0, 64, place, 0, unroll=8)
     gather(0)
     prev_top = None
     for b in range(NB + 1):
         peak = None
         if b < NB:
-            if b == 3:
+            if b == 2:
                 load_tail.wait()
             for group, (first, last) in enumerate(GROUPS):
                 if b == first:
-                    for member in range(first, last):
-                        for load in loads[member]:
-                            load.wait()
+                    for load in loads[group]:
+                        load.wait()
                     if group + AHEAD < len(GROUPS):
                         start(group + AHEAD)
-            if b in (3, 6, 10):
-                gather({3: 1, 6: 2, 10: 3}[b])
+            if b in (2, 6, 8):
+                gather({2: 1, 6: 2, 8: 3}[b])
             q = qs[b]
         if b > 0:
             acc = total = None
@@ -258,7 +282,7 @@
     return pl.pallas_call(
         prefix_kernel,
         out_shape=jax.ShapeDtypeStruct((DEST, ROWS, 128), BF),
-        in_specs=[SMEM, VMEM, ANY, ANY, ANY],
+        in_specs=[VMEM, VMEM, ANY, ANY, ANY],
         out_specs=ANY,
         scratch_shapes=[
             pltpu.VMEM((NB, 256, 128), BF),
@@ -268,8 +292,8 @@
             pltpu.VMEM((2, KVH, 4, 128), F32),
             pltpu.VMEM((DEST, 32, 128), F32),
             pltpu.VMEM((DEST, ROWS, 128), BF),
-            pltpu.SMEM((64,), jnp.int32),
-            pltpu.SMEM((PROMPTS,), jnp.int32),
+            pltpu.VMEM((64, HEADS * HD), F32),
+            pltpu.VMEM((64, HEADS * HD), BF),
             pltpu.SemaphoreType.DMA,
             pltpu.SemaphoreType.DMA((NB,)),
             pltpu.SemaphoreType.DMA((NB,)),
@@ -305,7 +329,7 @@
 
 def project_kernel(r_ref, pm_ref, un_ref, w_hbm, z_ref, wv, yv, zf, wsem):
     loads = [pltpu.make_async_copy(w_hbm.at[n], wv.at[n], wsem.at[n]) for n in range(8)]
-    for load in loads:
+    for load in loads[:4]:
         load.start()
     f = lambda x: x.astype(F32)
     lane = iota((256, 128), 1)
@@ -323,6 +347,10 @@
         term = jnp.where(lane == (row & 15), term, 0.0).sum(1, keepdims=True)
         terms = terms + jnp.where(lane == n, jnp.broadcast_to(term, (256, 128)), 0.0)
     moved = dot(pm_ref[...], jnp.concatenate([cont, terms.astype(BF)], 1))
+    for load in loads[:4]:
+        load.wait()
+    for load in loads[4:]:
+        load.start()
     log_c = moved[:, 128:129] + moved[:, 129:130] + moved[:, 130:131]
     top = jnp.maximum(jnp.where(lane < 16, logs, -jnp.inf).max(1, keepdims=True), log_c)
     w_c = jnp.exp2(log_c - top)
@@ -336,9 +364,10 @@
     mixed = dot(un_ref[...], mixed).astype(BF)
     member = lax.axis_index("group")
     z, core = member >> 1, member & 1
-    for load in loads:
-        load.wait()
     for n in range(8):
+        if n == 4:
+            for load in loads[4:]:
+                load.wait()
         g = 2 * ((z - n % 4) & 3) + (core if n < 4 else 1 - core)
         yv[g] = dot(mixed, wv[n])
     for g in range(8):
@@ -398,12 +427,11 @@
 def per_device(
     queries, prefix_keys, prefix_values, cont_keys, cont_values, cont_len, prompt_of, w_out
 ):
-    q_rows = queries.reshape(4 * HEADS, HD)
-    copies = jnp.broadcast_to(q_rows[None], (DEST, 4 * HEADS, HD))
+    copies = copies_call(queries)
     copies, w_out = lax.optimization_barrier((copies, w_out))
-    gathered = lax.all_to_all(copies, "seq", 0, 0).reshape(64, KVH, 16, HD)
+    gathered = lax.all_to_all(copies, "seq", 0, 0)
     weights = gather_weights(w_out, lax.axis_index("seq"))
-    tail, pm, unsort = cont_call(cont_len[0], prompt_of, q_rows, cont_keys[0], cont_values[0])
+    tail, pm, unsort = cont_call(cont_len[0], prompt_of, queries, cont_keys[0], cont_values[0])
     part = prefix_call(prompt_of, gathered, tail, prefix_keys[0], prefix_values[0])
     part, weights = lax.optimization_barrier((part, weights))
     swap = [(j, j ^ 1) for j in range(8)]

time: 82.5 us -> 81.9 us (level)
  local copies, waits for them, and re-layouts: 5.26 us -> 3.04 us
  Pallas kernels: 26.7 us -> 27.9 us
  waiting for transfers between devices: 18.5 us -> 19.5 us
    broadcast_in_dim x2 -> x0, local copies, waits for them, and re-layouts: 2.2 us -> none  [per_device(): copies = jnp.broadcast_to(q_rows[None], (DEST, 4 * HEADS, HD))]
    pallas_call x0 -> x1, Pallas kernels: none -> 2.06 us  [copies_call(): pl.pallas_call(copies_kernel, out_shape=jax.ShapeDtypeStruct((DEST, 4, HE...]
    all_to_all x1, waiting for transfers between devices: 10.1 us -> 11 us  [per_device(): received = lax.all_to_all(part, 'seq', 0, 0)]
    unnamed x10 -> x8, local copies, waits for them, and re-layouts: 1.98 us -> 1.96 us
where the time goes in v3:
time: 81.9 us; the launch traced here: 81.4 us
  Pallas kernels  27.9 us (34%)
  waiting for transfers between devices  19.5 us (24%)
  starting transfers between devices  17.7 us (22%)
  blocking collectives  13.3 us (16%)
  local copies, waits for them, and re-layouts  3.04 us (4%)
    pallas_call x1, Pallas kernels, prefix_call(): pl.pallas_call(prefix_kernel, out_shape=jax.ShapeDtypeStruct((DEST, ROWS,...  14.8 us
    all_to_all x1, blocking collectives, per_device(): return sum_call(lax.all_to_all(y, 'seq', 0, 0))  13.3 us
    all_to_all x1, waiting for transfers between devices, per_device(): received = lax.all_to_all(part, 'seq', 0, 0)  11 us
    all_to_all x1, starting transfers between devices, per_device(): gathered = lax.all_to_all(copies, 'seq', 0, 0)  7.05 us
    ppermute x3, starting transfers between devices, gather_weights(): blocks.append(lax.ppermute(own, 'group', hop))  5.68 us
    pallas_call x1, Pallas kernels, cont_call(): pl.pallas_call(cont_kernel, out_shape=(jax.ShapeDtypeStruct((DEST, TAIL_P...  5.66 us
    all_to_all x1, waiting for transfers between devices, per_device(): gathered = lax.all_to_all(copies, 'seq', 0, 0)  5.26 us
    pallas_call x1, Pallas kernels, project_call(): pl.pallas_call(project_kernel, out_shape=jax.ShapeDtypeStruct((DEST, 16,...  4.3 us
  transfers between devices with their start and end apart: 9, of which 6 were waited for; matrix products, arithmetic and copies ran while one was open for 1% of the time, Pallas kernels for 26%

profile of v3, /device:TPU:32, one launch (start us, length us, event | category | flops | bytes accessed | tf_op | source)
XLA Modules:
  0.0 81.4 jit_solution(13450829842338332264)
XLA Ops:
  0.0 0.0 copy-start.3
  0.0 2.1 %copies.1 = bf16[16,4,8192]{2,1,0:T(4,128)(2,1)} custom-call(bf16[1,4,8192]{2,1,0:T(4,128)(2,1)} %q_in.1), custom_call_target="tpu_custom_call" | custom-call | tf_op jit(solution)/shard_map/copies/pallas_call | solution.py:61
  2.1 7.0 %all-to-all-start = ((bf16[16,4,8192]{2,1,0:T(4,128)(2,1)}), bf16[16,4,8192]{2,1,0:T(4,128)(2,1)S(1)}, u32[]{:S(2)}, u32[]{:S(2)}) async-start(bf16[16,4,8192]{2,1,0:T(4,128)(2,1)} %copies.1), calls=%async_computation | async-start | bytes 2097152 | tf_op jit(solution)/shard_map/all_to_all | solution.py:432
  9.1 1.1 %constant_dynamic-slice_fusion.refs_0_ = bf16[512,512]{1,0:T(8,128)(2,1)S(1)} fusion(bf16[8192,512]{1,0:T(8,128)(2,1)} %param.15, s32[]{:T(128)S(6)} %select_n.3), kind=kLoop, calls=%fused_computation | loop fusion | bytes 1048580 | tf_op jit(solution)/shard_map/dynamic_slice | solution.py:419
  10.2 2.0 %collective-permute-start = (bf16[512,512]{1,0:T(8,128)(2,1)S(1)}, bf16[512,512]{1,0:T(8,128)(2,1)S(1)}, u32[]{:S(2)}, u32[]{:S(2)}) collective-permute-start(bf16[512,512]{1,0:T(8,128)(2,1)S(1)} %constant_dynamic-slice_fusion.refs_0_), channel_id=1, source_target_pairs={{0,32},{16,48},{32,64},{48,80},{64,96},{80,112},{96,0},{112,16},{1... | collective-permute-start | bytes 1572872 | tf_op jit(solution)/shard_map/ppermute | solution.py:423
  12.2 1.2 %collective-permute-start.1 = (bf16[512,512]{1,0:T(8,128)(2,1)S(1)}, bf16[512,512]{1,0:T(8,128)(2,1)S(1)}, u32[]{:S(2)}, u32[]{:S(2)}) collective-permute-start(bf16[512,512]{1,0:T(8,128)(2,1)S(1)} %constant_dynamic-slice_fusion.refs_0_), channel_id=1, source_target_pairs={{0,64},{16,80},{32,96},{48,112},{64,0},{80,16},{96,32},{112,48},{1... | collective-permute-start | bytes 1572872 | tf_op jit(solution)/shard_map/ppermute | solution.py:423
  13.3 2.5 %collective-permute-start.2 = (bf16[512,512]{1,0:T(8,128)(2,1)S(1)}, bf16[512,512]{1,0:T(8,128)(2,1)S(1)}, u32[]{:S(2)}, u32[]{:S(2)}) collective-permute-start(bf16[512,512]{1,0:T(8,128)(2,1)S(1)} %constant_dynamic-slice_fusion.refs_0_), channel_id=1, source_target_pairs={{0,96},{16,112},{32,0},{48,16},{64,32},{80,48},{96,64},{112,80},{1... | collective-permute-start | bytes 1572872 | tf_op jit(solution)/shard_map/ppermute | solution.py:423
  15.9 5.7 %cont.1 = (f32[16,1024,128]{2,1,0:T(8,128)}, bf16[256,256]{1,0:T(8,128)(2,1)}, bf16[64,64]{1,0:T(8,128)(2,1)}) custom-call(s32[4]{0:T(128)} %bitcast.9, s32[1,64]{1,0:T(1,128)} %prompt.1, bf16[1,4,8192]{2,1,0:T(4,128)(2,1)} %q_in.1, bf16[4,4,512,128]{3,2,1,0:T(8,128)(2,1)} %bitcast.7, bf16[4,4,512,128]{3,2,1,0:T(8,128)(2,1)} %bitcast.8), custom_call_target="tpu_custom_call" | custom-call | flops 2000000000 | bytes 4194304 | tf_op jit(solution)/shard_map/cont/pallas_call | solution.py:145
  21.6 5.3 %all-to-all-done.q_ref = bf16[16,4,8192]{2,1,0:T(4,128)(2,1)S(1)} async-done(((bf16[16,4,8192]{2,1,0:T(4,128)(2,1)}), bf16[16,4,8192]{2,1,0:T(4,128)(2,1)S(1)}, u32[]{:S(2)}, u32[]{:S(2)}) %all-to-all-start) | async-done | bytes 1048608 | tf_op jit(solution)/shard_map/all_to_all | solution.py:432
  26.8 0.0 copy-done.3
  26.8 14.8 %prefix.1 = bf16[16,288,128]{2,1,0:T(8,128)(2,1)} custom-call(s32[1,64]{1,0:T(1,128)S(1)} %copy-done.3, bf16[16,4,8192]{2,1,0:T(4,128)(2,1)S(1)} %all-to-all-done.q_ref, f32[16,1024,128]{2,1,0:T(8,128)} %get-tuple-element.16.tail_hbm, bf16[4,4,2048,128]{3,2,1,0:T(8,128)(2,1)} %bitcast.5, bf16[4,4,2048,128]{3,2,1,0:T(8,128)(2,1)} %bitcast.6), custom_call_target="tpu_custom_call" | custom-call | flops 8999999488 | bytes 18874368 | tf_op jit(solution)/shard_map/prefix/pallas_call | solution.py:282
  41.6 0.0 copy-start.1
  41.6 0.0 copy-start.2
  41.6 0.0 collective-permute-done.refs_1_
  41.7 0.0 collective-permute-done.1.refs_2_
  41.7 0.0 collective-permute-done.2.refs_3_
  41.7 3.8 %all-to-all-start.1 = ((bf16[16,288,128]{2,1,0:T(8,128)(2,1)}), bf16[16,288,128]{2,1,0:T(8,128)(2,1)S(1)}, u32[]{:S(2)}, u32[]{:S(2)}) async-start(bf16[16,288,128]{2,1,0:T(8,128)(2,1)} %prefix.1), calls=%async_computation.1 | async-start | bytes 2359296 | tf_op jit(solution)/shard_map/all_to_all | solution.py:439
  45.5 0.1 collective-permute-start.3
  45.6 0.5 collective-permute-start.4
  46.1 0.1 collective-permute-start.5
  46.2 0.4 collective-permute-start.6
  46.6 0.9 %collective-permute-done.3.refs_4_ = bf16[512,512]{1,0:T(8,128)(2,1)S(1)} collective-permute-done((bf16[512,512]{1,0:T(8,128)(2,1)S(1)}, bf16[512,512]{1,0:T(8,128)(2,1)S(1)}, u32[]{:S(2)}, u32[]{:S(2)}) %collective-permute-start.3) | collective-permute-done | bytes 524320 | tf_op jit(solution)/shard_map/ppermute | solution.py:438
  47.5 0.7 collective-permute-done.4.refs_5_
  48.3 0.7 collective-permute-done.5.refs_6_
  49.0 0.7 collective-permute-done.6.refs_7_
  49.8 0.4 pack.1.w_hbm
  50.1 0.0 copy-start
  50.1 1.9 %copy-done = bf16[8,512,512]{2,1,0:T(8,128)(2,1)} copy-done((bf16[8,512,512]{2,1,0:T(8,128)(2,1)}, bf16[8,512,512]{2,1,0:T(8,128)(2,1)S(1)}, u32[]{:S(2)}) %copy-start) | copy-done | bytes 4194328
  52.1 11.0 %all-to-all-done.1.r_ref = bf16[16,288,128]{2,1,0:T(8,128)(2,1)S(1)} async-done(((bf16[16,288,128]{2,1,0:T(8,128)(2,1)}), bf16[16,288,128]{2,1,0:T(8,128)(2,1)S(1)}, u32[]{:S(2)}, u32[]{:S(2)}) %all-to-all-start.1) | async-done | bytes 1179680 | tf_op jit(solution)/shard_map/all_to_all | solution.py:439
  63.1 0.0 copy-done.1
  63.1 0.0 copy-done.2
  63.1 4.3 %project.1 = bf16[16,16,1024]{2,1,0:T(8,128)(2,1)S(1)} custom-call(bf16[16,288,128]{2,1,0:T(8,128)(2,1)S(1)} %all-to-all-done.1.r_ref, bf16[256,256]{1,0:T(8,128)(2,1)S(1)} %copy-done.1, bf16[64,64]{1,0:T(8,128)(2,1)S(1)} %copy-done.2, bf16[8,512,512]{2,1,0:T(8,128)(2,1)} %copy-done), custom_call_target="tpu_custom_call" | custom-call | flops 300000000 | bytes 4194304 | tf_op jit(solution)/shard_map/project/pallas_call | solution.py:380
  67.5 13.3 %all_to_all.15.r_ref = bf16[16,16,1024]{2,1,0:T(8,128)(2,1)S(1)} all-to-all(bf16[16,16,1024]{2,1,0:T(8,128)(2,1)S(1)} %project.1), channel_id=1, replica_groups=mesh['group'=8,'seq'=16] {'seq'}, dimensions={0} | all-to-all | bytes 1048576 | tf_op jit(solution)/shard_map/all_to_all | solution.py:441
  80.8 0.7 sum.1
Async XLA Ops:
  0.0 26.8 %copy-start.3 = (s32[1,64]{1,0:T(1,128)S(1)}, s32[1,64]{1,0:T(1,128)}, u32[]{:S(2)}) copy-start(s32[1,64]{1,0:T(1,128)} %prompt.1) | copy-start | bytes 772
  2.1 24.8 %all-to-all-start = ((bf16[16,4,8192]{2,1,0:T(4,128)(2,1)}), bf16[16,4,8192]{2,1,0:T(4,128)(2,1)S(1)}, u32[]{:S(2)}, u32[]{:S(2)}) async-start(bf16[16,4,8192]{2,1,0:T(4,128)(2,1)} %copies.1), calls=%async_computation | async-start | bytes 2097152 | tf_op jit(solution)/shard_map/all_to_all | solution.py:432
  10.2 31.4 %collective-permute-start = (bf16[512,512]{1,0:T(8,128)(2,1)S(1)}, bf16[512,512]{1,0:T(8,128)(2,1)S(1)}, u32[]{:S(2)}, u32[]{:S(2)}) collective-permute-start(bf16[512,512]{1,0:T(8,128)(2,1)S(1)} %constant_dynamic-slice_fusion.refs_0_), channel_id=1, source_target_pairs={{0,32},{16,48},{32,64},{48,80},{64,96},{80,112},{96,0},{112,16},{1... | collective-permute-start | bytes 1572872 | tf_op jit(solution)/shard_map/ppermute | solution.py:423
  12.2 29.5 %collective-permute-start.1 = (bf16[512,512]{1,0:T(8,128)(2,1)S(1)}, bf16[512,512]{1,0:T(8,128)(2,1)S(1)}, u32[]{:S(2)}, u32[]{:S(2)}) collective-permute-start(bf16[512,512]{1,0:T(8,128)(2,1)S(1)} %constant_dynamic-slice_fusion.refs_0_), channel_id=1, source_target_pairs={{0,64},{16,80},{32,96},{48,112},{64,0},{80,16},{96,32},{112,48},{1... | collective-permute-start | bytes 1572872 | tf_op jit(solution)/shard_map/ppermute | solution.py:423
  13.3 28.3 %collective-permute-start.2 = (bf16[512,512]{1,0:T(8,128)(2,1)S(1)}, bf16[512,512]{1,0:T(8,128)(2,1)S(1)}, u32[]{:S(2)}, u32[]{:S(2)}) collective-permute-start(bf16[512,512]{1,0:T(8,128)(2,1)S(1)} %constant_dynamic-slice_fusion.refs_0_), channel_id=1, source_target_pairs={{0,96},{16,112},{32,0},{48,16},{64,32},{80,48},{96,64},{112,80},{1... | collective-permute-start | bytes 1572872 | tf_op jit(solution)/shard_map/ppermute | solution.py:423
  41.6 21.5 %copy-start.1 = (bf16[256,256]{1,0:T(8,128)(2,1)S(1)}, bf16[256,256]{1,0:T(8,128)(2,1)}, u32[]{:S(2)}) copy-start(bf16[256,256]{1,0:T(8,128)(2,1)} %get-tuple-element.19.pm_ref) | copy-start | bytes 393220
  41.6 21.5 %copy-start.2 = (bf16[64,64]{1,0:T(8,128)(2,1)S(1)}, bf16[64,64]{1,0:T(8,128)(2,1)}, u32[]{:S(2)}) copy-start(bf16[64,64]{1,0:T(8,128)(2,1)} %get-tuple-element.20.un_ref) | copy-start | bytes 24580
  41.7 21.5 %all-to-all-start.1 = ((bf16[16,288,128]{2,1,0:T(8,128)(2,1)}), bf16[16,288,128]{2,1,0:T(8,128)(2,1)S(1)}, u32[]{:S(2)}, u32[]{:S(2)}) async-start(bf16[16,288,128]{2,1,0:T(8,128)(2,1)} %prefix.1), calls=%async_computation.1 | async-start | bytes 2359296 | tf_op jit(solution)/shard_map/all_to_all | solution.py:439
  45.5 2.0 %collective-permute-start.3 = (bf16[512,512]{1,0:T(8,128)(2,1)S(1)}, bf16[512,512]{1,0:T(8,128)(2,1)S(1)}, u32[]{:S(2)}, u32[]{:S(2)}) collective-permute-start(bf16[512,512]{1,0:T(8,128)(2,1)S(1)} %constant_dynamic-slice_fusion.refs_0_), channel_id=1, source_target_pairs={{0,16},{16,0},{32,48},{48,32},{64,80},{80,64},{96,112},{112,96},{1... | collective-permute-start | bytes 1572872 | tf_op jit(solution)/shard_map/ppermute | solution.py:438
  45.6 2.6 %collective-permute-start.4 = (bf16[512,512]{1,0:T(8,128)(2,1)S(1)}, bf16[512,512]{1,0:T(8,128)(2,1)S(1)}, u32[]{:S(2)}, u32[]{:S(2)}) collective-permute-start(bf16[512,512]{1,0:T(8,128)(2,1)S(1)} %collective-permute-done.refs_1_), channel_id=1, source_target_pairs={{0,16},{16,0},{32,48},{48,32},{64,80},{80,64},{96,112},{112,96},{1... | collective-permute-start | bytes 1572872 | tf_op jit(solution)/shard_map/ppermute | solution.py:438
  46.1 2.9 %collective-permute-start.5 = (bf16[512,512]{1,0:T(8,128)(2,1)S(1)}, bf16[512,512]{1,0:T(8,128)(2,1)S(1)}, u32[]{:S(2)}, u32[]{:S(2)}) collective-permute-start(bf16[512,512]{1,0:T(8,128)(2,1)S(1)} %collective-permute-done.1.refs_2_), channel_id=1, source_target_pairs={{0,16},{16,0},{32,48},{48,32},{64,80},{80,64},{96,112},{112,96},{1... | collective-permute-start | bytes 1572872 | tf_op jit(solution)/shard_map/ppermute | solution.py:438
  46.2 3.6 %collective-permute-start.6 = (bf16[512,512]{1,0:T(8,128)(2,1)S(1)}, bf16[512,512]{1,0:T(8,128)(2,1)S(1)}, u32[]{:S(2)}, u32[]{:S(2)}) collective-permute-start(bf16[512,512]{1,0:T(8,128)(2,1)S(1)} %collective-permute-done.2.refs_3_), channel_id=1, source_target_pairs={{0,16},{16,0},{32,48},{48,32},{64,80},{80,64},{96,112},{112,96},{1... | collective-permute-start | bytes 1572872 | tf_op jit(solution)/shard_map/ppermute | solution.py:438
  50.1 2.0 %copy-start = (bf16[8,512,512]{2,1,0:T(8,128)(2,1)}, bf16[8,512,512]{2,1,0:T(8,128)(2,1)S(1)}, u32[]{:S(2)}) copy-start(bf16[8,512,512]{2,1,0:T(8,128)(2,1)S(1)} %pack.1.w_hbm) | copy-start | bytes 12582916

commit v4 on v3

--- a/solution.py
+++ b/solution.py
@@ -264,7 +264,7 @@
                     piece = s[:, 128 * z : 128 * z + 128]
                     peak = piece if peak is None else jnp.maximum(peak, piece)
             if b > 0:
-                w = jnp.exp2((sbuf[(b - 1) % 2, :, cols] - prev_top) * SCALE2)
+                w = jnp.exp2(sbuf[(b - 1) % 2, :, cols] * SCALE2 - prev_peak)
                 for z in range(TC // 128):
                     piece = w[:, 128 * z : 128 * z + 128]
                     total = piece if total is None else total + piece
@@ -274,6 +274,7 @@
             finish(b - 1, acc, prev_top, total.sum(1, keepdims=True))
         if b < NB:
             prev_top = peak.max(1, keepdims=True)
+            prev_peak = prev_top * SCALE2
     for send in sends:
         send.wait()
 

time: 81.9 us -> 82.6 us (level)
  Pallas kernels: 27.9 us -> 29 us
  waiting for transfers between devices: 19.5 us -> 18.5 us
    pallas_call x1, Pallas kernels: 14.8 us -> 15.9 us  [prefix_call(): pl.pallas_call(prefix_kernel, out_shape=jax.ShapeDtypeStruct((DEST, ROWS,...]
    all_to_all x1, waiting for transfers between devices: 11 us -> 10.1 us  [per_device(): received = lax.all_to_all(part, 'seq', 0, 0)]
  transfers between devices with their start and end apart: 9 -> 9, of which waited for: 6 -> 6; matrix products, arithmetic and copies ran while one was open for 1% -> 1% of each run, Pallas kernels for 26% -> 27%
where the time goes in v4:
time: 82.6 us; the launch traced here: 82.1 us
  Pallas kernels  29 us (35%)
  waiting for transfers between devices  18.5 us (22%)
  starting transfers between devices  17.7 us (21%)
  blocking collectives  13.8 us (17%)
  local copies, waits for them, and re-layouts  3.04 us (4%)
    pallas_call x1, Pallas kernels, prefix_call(): pl.pallas_call(prefix_kernel, out_shape=jax.ShapeDtypeStruct((DEST, ROWS,...  15.9 us
    all_to_all x1, blocking collectives, per_device(): return sum_call(lax.all_to_all(y, 'seq', 0, 0))  13.8 us
    all_to_all x1, waiting for transfers between devices, per_device(): received = lax.all_to_all(part, 'seq', 0, 0)  10.1 us
    all_to_all x1, starting transfers between devices, per_device(): gathered = lax.all_to_all(copies, 'seq', 0, 0)  7.05 us
    ppermute x3, starting transfers between devices, gather_weights(): blocks.append(lax.ppermute(own, 'group', hop))  5.68 us
    pallas_call x1, Pallas kernels, cont_call(): pl.pallas_call(cont_kernel, out_shape=(jax.ShapeDtypeStruct((DEST, TAIL_P...  5.66 us
    all_to_all x1, waiting for transfers between devices, per_device(): gathered = lax.all_to_all(copies, 'seq', 0, 0)  5.26 us
    pallas_call x1, Pallas kernels, project_call(): pl.pallas_call(project_kernel, out_shape=jax.ShapeDtypeStruct((DEST, 16,...  4.3 us
  transfers between devices with their start and end apart: 9, of which 6 were waited for; matrix products, arithmetic and copies ran while one was open for 1% of the time, Pallas kernels for 27%

profile of v4, /device:TPU:32, one launch (start us, length us, event | category | flops | bytes accessed | tf_op | source)
XLA Modules:
  0.0 82.1 jit_solution(6833204407533982730)
XLA Ops:
  0.0 0.0 copy-start.3
  0.0 2.1 %copies.1 = bf16[16,4,8192]{2,1,0:T(4,128)(2,1)} custom-call(bf16[1,4,8192]{2,1,0:T(4,128)(2,1)} %q_in.1), custom_call_target="tpu_custom_call" | custom-call | tf_op jit(solution)/shard_map/copies/pallas_call | solution.py:61
  2.1 7.0 %all-to-all-start = ((bf16[16,4,8192]{2,1,0:T(4,128)(2,1)}), bf16[16,4,8192]{2,1,0:T(4,128)(2,1)S(1)}, u32[]{:S(2)}, u32[]{:S(2)}) async-start(bf16[16,4,8192]{2,1,0:T(4,128)(2,1)} %copies.1), calls=%async_computation | async-start | bytes 2097152 | tf_op jit(solution)/shard_map/all_to_all | solution.py:433
  9.1 1.1 %constant_dynamic-slice_fusion.refs_0_ = bf16[512,512]{1,0:T(8,128)(2,1)S(1)} fusion(bf16[8192,512]{1,0:T(8,128)(2,1)} %param.15, s32[]{:T(128)S(6)} %select_n.3), kind=kLoop, calls=%fused_computation | loop fusion | bytes 1048580 | tf_op jit(solution)/shard_map/dynamic_slice | solution.py:420
  10.2 2.0 %collective-permute-start = (bf16[512,512]{1,0:T(8,128)(2,1)S(1)}, bf16[512,512]{1,0:T(8,128)(2,1)S(1)}, u32[]{:S(2)}, u32[]{:S(2)}) collective-permute-start(bf16[512,512]{1,0:T(8,128)(2,1)S(1)} %constant_dynamic-slice_fusion.refs_0_), channel_id=1, source_target_pairs={{0,32},{16,48},{32,64},{48,80},{64,96},{80,112},{96,0},{112,16},{1... | collective-permute-start | bytes 1572872 | tf_op jit(solution)/shard_map/ppermute | solution.py:424
  12.2 1.2 %collective-permute-start.1 = (bf16[512,512]{1,0:T(8,128)(2,1)S(1)}, bf16[512,512]{1,0:T(8,128)(2,1)S(1)}, u32[]{:S(2)}, u32[]{:S(2)}) collective-permute-start(bf16[512,512]{1,0:T(8,128)(2,1)S(1)} %constant_dynamic-slice_fusion.refs_0_), channel_id=1, source_target_pairs={{0,64},{16,80},{32,96},{48,112},{64,0},{80,16},{96,32},{112,48},{1... | collective-permute-start | bytes 1572872 | tf_op jit(solution)/shard_map/ppermute | solution.py:424
  13.3 2.5 %collective-permute-start.2 = (bf16[512,512]{1,0:T(8,128)(2,1)S(1)}, bf16[512,512]{1,0:T(8,128)(2,1)S(1)}, u32[]{:S(2)}, u32[]{:S(2)}) collective-permute-start(bf16[512,512]{1,0:T(8,128)(2,1)S(1)} %constant_dynamic-slice_fusion.refs_0_), channel_id=1, source_target_pairs={{0,96},{16,112},{32,0},{48,16},{64,32},{80,48},{96,64},{112,80},{1... | collective-permute-start | bytes 1572872 | tf_op jit(solution)/shard_map/ppermute | solution.py:424
  15.9 5.7 %cont.1 = (f32[16,1024,128]{2,1,0:T(8,128)}, bf16[256,256]{1,0:T(8,128)(2,1)}, bf16[64,64]{1,0:T(8,128)(2,1)}) custom-call(s32[4]{0:T(128)} %bitcast.9, s32[1,64]{1,0:T(1,128)} %prompt.1, bf16[1,4,8192]{2,1,0:T(4,128)(2,1)} %q_in.1, bf16[4,4,512,128]{3,2,1,0:T(8,128)(2,1)} %bitcast.7, bf16[4,4,512,128]{3,2,1,0:T(8,128)(2,1)} %bitcast.8), custom_call_target="tpu_custom_call" | custom-call | flops 2000000000 | bytes 4194304 | tf_op jit(solution)/shard_map/cont/pallas_call | solution.py:145
  21.6 5.3 %all-to-all-done.q_ref = bf16[16,4,8192]{2,1,0:T(4,128)(2,1)S(1)} async-done(((bf16[16,4,8192]{2,1,0:T(4,128)(2,1)}), bf16[16,4,8192]{2,1,0:T(4,128)(2,1)S(1)}, u32[]{:S(2)}, u32[]{:S(2)}) %all-to-all-start) | async-done | bytes 1048608 | tf_op jit(solution)/shard_map/all_to_all | solution.py:433
  26.8 0.0 copy-done.3
  26.8 15.9 %prefix.1 = bf16[16,288,128]{2,1,0:T(8,128)(2,1)} custom-call(s32[1,64]{1,0:T(1,128)S(1)} %copy-done.3, bf16[16,4,8192]{2,1,0:T(4,128)(2,1)S(1)} %all-to-all-done.q_ref, f32[16,1024,128]{2,1,0:T(8,128)} %get-tuple-element.16.tail_hbm, bf16[4,4,2048,128]{3,2,1,0:T(8,128)(2,1)} %bitcast.5, bf16[4,4,2048,128]{3,2,1,0:T(8,128)(2,1)} %bitcast.6), custom_call_target="tpu_custom_call" | custom-call | flops 8999999488 | bytes 18874368 | tf_op jit(solution)/shard_map/prefix/pallas_call | solution.py:283
  42.7 0.0 copy-start.1
  42.7 0.0 copy-start.2
  42.8 0.0 collective-permute-done.refs_1_
  42.8 0.0 collective-permute-done.1.refs_2_
  42.8 0.0 collective-permute-done.2.refs_3_
  42.8 3.8 %all-to-all-start.1 = ((bf16[16,288,128]{2,1,0:T(8,128)(2,1)}), bf16[16,288,128]{2,1,0:T(8,128)(2,1)S(1)}, u32[]{:S(2)}, u32[]{:S(2)}) async-start(bf16[16,288,128]{2,1,0:T(8,128)(2,1)} %prefix.1), calls=%async_computation.1 | async-start | bytes 2359296 | tf_op jit(solution)/shard_map/all_to_all | solution.py:440
  46.6 0.1 collective-permute-start.3
  46.7 0.5 collective-permute-start.4
  47.2 0.1 collective-permute-start.5
  47.3 0.4 collective-permute-start.6
  47.7 0.9 %collective-permute-done.3.refs_4_ = bf16[512,512]{1,0:T(8,128)(2,1)S(1)} collective-permute-done((bf16[512,512]{1,0:T(8,128)(2,1)S(1)}, bf16[512,512]{1,0:T(8,128)(2,1)S(1)}, u32[]{:S(2)}, u32[]{:S(2)}) %collective-permute-start.3) | collective-permute-done | bytes 524320 | tf_op jit(solution)/shard_map/ppermute | solution.py:439
  48.6 0.7 collective-permute-done.4.refs_5_
  49.4 0.7 collective-permute-done.5.refs_6_
  50.1 0.7 collective-permute-done.6.refs_7_
  50.9 0.4 pack.1.w_hbm
  51.3 0.0 copy-start
  51.3 1.9 %copy-done = bf16[8,512,512]{2,1,0:T(8,128)(2,1)} copy-done((bf16[8,512,512]{2,1,0:T(8,128)(2,1)}, bf16[8,512,512]{2,1,0:T(8,128)(2,1)S(1)}, u32[]{:S(2)}) %copy-start) | copy-done | bytes 4194328
  53.2 10.1 %all-to-all-done.1.r_ref = bf16[16,288,128]{2,1,0:T(8,128)(2,1)S(1)} async-done(((bf16[16,288,128]{2,1,0:T(8,128)(2,1)}), bf16[16,288,128]{2,1,0:T(8,128)(2,1)S(1)}, u32[]{:S(2)}, u32[]{:S(2)}) %all-to-all-start.1) | async-done | bytes 1179680 | tf_op jit(solution)/shard_map/all_to_all | solution.py:440
  63.3 0.0 copy-done.1
  63.3 0.0 copy-done.2
  63.3 4.3 %project.1 = bf16[16,16,1024]{2,1,0:T(8,128)(2,1)S(1)} custom-call(bf16[16,288,128]{2,1,0:T(8,128)(2,1)S(1)} %all-to-all-done.1.r_ref, bf16[256,256]{1,0:T(8,128)(2,1)S(1)} %copy-done.1, bf16[64,64]{1,0:T(8,128)(2,1)S(1)} %copy-done.2, bf16[8,512,512]{2,1,0:T(8,128)(2,1)} %copy-done), custom_call_target="tpu_custom_call" | custom-call | flops 300000000 | bytes 4194304 | tf_op jit(solution)/shard_map/project/pallas_call | solution.py:381
  67.6 13.8 %all_to_all.15.r_ref = bf16[16,16,1024]{2,1,0:T(8,128)(2,1)S(1)} all-to-all(bf16[16,16,1024]{2,1,0:T(8,128)(2,1)S(1)} %project.1), channel_id=1, replica_groups=mesh['group'=8,'seq'=16] {'seq'}, dimensions={0} | all-to-all | bytes 1048576 | tf_op jit(solution)/shard_map/all_to_all | solution.py:442
  81.4 0.7 sum.1
Async XLA Ops:
  0.0 26.8 %copy-start.3 = (s32[1,64]{1,0:T(1,128)S(1)}, s32[1,64]{1,0:T(1,128)}, u32[]{:S(2)}) copy-start(s32[1,64]{1,0:T(1,128)} %prompt.1) | copy-start | bytes 772
  2.1 24.8 %all-to-all-start = ((bf16[16,4,8192]{2,1,0:T(4,128)(2,1)}), bf16[16,4,8192]{2,1,0:T(4,128)(2,1)S(1)}, u32[]{:S(2)}, u32[]{:S(2)}) async-start(bf16[16,4,8192]{2,1,0:T(4,128)(2,1)} %copies.1), calls=%async_computation | async-start | bytes 2097152 | tf_op jit(solution)/shard_map/all_to_all | solution.py:433
  10.2 32.6 %collective-permute-start = (bf16[512,512]{1,0:T(8,128)(2,1)S(1)}, bf16[512,512]{1,0:T(8,128)(2,1)S(1)}, u32[]{:S(2)}, u32[]{:S(2)}) collective-permute-start(bf16[512,512]{1,0:T(8,128)(2,1)S(1)} %constant_dynamic-slice_fusion.refs_0_), channel_id=1, source_target_pairs={{0,32},{16,48},{32,64},{48,80},{64,96},{80,112},{96,0},{112,16},{1... | collective-permute-start | bytes 1572872 | tf_op jit(solution)/shard_map/ppermute | solution.py:424
  12.2 30.6 %collective-permute-start.1 = (bf16[512,512]{1,0:T(8,128)(2,1)S(1)}, bf16[512,512]{1,0:T(8,128)(2,1)S(1)}, u32[]{:S(2)}, u32[]{:S(2)}) collective-permute-start(bf16[512,512]{1,0:T(8,128)(2,1)S(1)} %constant_dynamic-slice_fusion.refs_0_), channel_id=1, source_target_pairs={{0,64},{16,80},{32,96},{48,112},{64,0},{80,16},{96,32},{112,48},{1... | collective-permute-start | bytes 1572872 | tf_op jit(solution)/shard_map/ppermute | solution.py:424
  13.3 29.4 %collective-permute-start.2 = (bf16[512,512]{1,0:T(8,128)(2,1)S(1)}, bf16[512,512]{1,0:T(8,128)(2,1)S(1)}, u32[]{:S(2)}, u32[]{:S(2)}) collective-permute-start(bf16[512,512]{1,0:T(8,128)(2,1)S(1)} %constant_dynamic-slice_fusion.refs_0_), channel_id=1, source_target_pairs={{0,96},{16,112},{32,0},{48,16},{64,32},{80,48},{96,64},{112,80},{1... | collective-permute-start | bytes 1572872 | tf_op jit(solution)/shard_map/ppermute | solution.py:424
  42.7 20.6 %copy-start.1 = (bf16[256,256]{1,0:T(8,128)(2,1)S(1)}, bf16[256,256]{1,0:T(8,128)(2,1)}, u32[]{:S(2)}) copy-start(bf16[256,256]{1,0:T(8,128)(2,1)} %get-tuple-element.19.pm_ref) | copy-start | bytes 393220
  42.7 20.6 %copy-start.2 = (bf16[64,64]{1,0:T(8,128)(2,1)S(1)}, bf16[64,64]{1,0:T(8,128)(2,1)}, u32[]{:S(2)}) copy-start(bf16[64,64]{1,0:T(8,128)(2,1)} %get-tuple-element.20.un_ref) | copy-start | bytes 24580
  42.8 20.5 %all-to-all-start.1 = ((bf16[16,288,128]{2,1,0:T(8,128)(2,1)}), bf16[16,288,128]{2,1,0:T(8,128)(2,1)S(1)}, u32[]{:S(2)}, u32[]{:S(2)}) async-start(bf16[16,288,128]{2,1,0:T(8,128)(2,1)} %prefix.1), calls=%async_computation.1 | async-start | bytes 2359296 | tf_op jit(solution)/shard_map/all_to_all | solution.py:440
  46.6 2.0 %collective-permute-start.3 = (bf16[512,512]{1,0:T(8,128)(2,1)S(1)}, bf16[512,512]{1,0:T(8,128)(2,1)S(1)}, u32[]{:S(2)}, u32[]{:S(2)}) collective-permute-start(bf16[512,512]{1,0:T(8,128)(2,1)S(1)} %constant_dynamic-slice_fusion.refs_0_), channel_id=1, source_target_pairs={{0,16},{16,0},{32,48},{48,32},{64,80},{80,64},{96,112},{112,96},{1... | collective-permute-start | bytes 1572872 | tf_op jit(solution)/shard_map/ppermute | solution.py:439
  46.7 2.6 %collective-permute-start.4 = (bf16[512,512]{1,0:T(8,128)(2,1)S(1)}, bf16[512,512]{1,0:T(8,128)(2,1)S(1)}, u32[]{:S(2)}, u32[]{:S(2)}) collective-permute-start(bf16[512,512]{1,0:T(8,128)(2,1)S(1)} %collective-permute-done.refs_1_), channel_id=1, source_target_pairs={{0,16},{16,0},{32,48},{48,32},{64,80},{80,64},{96,112},{112,96},{1... | collective-permute-start | bytes 1572872 | tf_op jit(solution)/shard_map/ppermute | solution.py:439
  47.2 2.9 %collective-permute-start.5 = (bf16[512,512]{1,0:T(8,128)(2,1)S(1)}, bf16[512,512]{1,0:T(8,128)(2,1)S(1)}, u32[]{:S(2)}, u32[]{:S(2)}) collective-permute-start(bf16[512,512]{1,0:T(8,128)(2,1)S(1)} %collective-permute-done.1.refs_2_), channel_id=1, source_target_pairs={{0,16},{16,0},{32,48},{48,32},{64,80},{80,64},{96,112},{112,96},{1... | collective-permute-start | bytes 1572872 | tf_op jit(solution)/shard_map/ppermute | solution.py:439
  47.3 3.6 %collective-permute-start.6 = (bf16[512,512]{1,0:T(8,128)(2,1)S(1)}, bf16[512,512]{1,0:T(8,128)(2,1)S(1)}, u32[]{:S(2)}, u32[]{:S(2)}) collective-permute-start(bf16[512,512]{1,0:T(8,128)(2,1)S(1)} %collective-permute-done.2.refs_3_), channel_id=1, source_target_pairs={{0,16},{16,0},{32,48},{48,32},{64,80},{80,64},{96,112},{112,96},{1... | collective-permute-start | bytes 1572872 | tf_op jit(solution)/shard_map/ppermute | solution.py:439
  51.3 2.0 %copy-start = (bf16[8,512,512]{2,1,0:T(8,128)(2,1)}, bf16[8,512,512]{2,1,0:T(8,128)(2,1)S(1)}, u32[]{:S(2)}) copy-start(bf16[8,512,512]{2,1,0:T(8,128)(2,1)S(1)} %pack.1.w_hbm) | copy-start | bytes 12582916
